TPU v7x, 32 devices: a whole 2x2x4 slice. The times are simulated.
32 devices in a mesh: fsdp: 8 (over z, y), tp: 4 (over x, core).
Axes of the slice: x: 2, y: 2, z: 4, core: 2. Of those that a mesh axis runs over, the one named last changes fastest.
Arguments:
- hidden_in: bfloat16 [8, 4, 256, 1152], P('fsdp', 'tp'), may hold values from -6 to 6
- cotangent: bfloat16 [8, 4, 256, 1152], P('fsdp', 'tp'), may hold values from -6 to 6
- image_group: int32 [12], replicated, may hold values from 0 to 7, never falling along the last dimension, each value on 1 to 2 neighbouring positions
- block_sizes: int32 [8, 4], P('fsdp'), may hold values from 1 to 256, 512 in all within a row
- joint_weight: bfloat16 [3, 1152, 1152], P(None, 'fsdp', 'tp'), may hold values from -0.25 to 0.25
- joint_bias: bfloat16 [2, 1152], P(None, 'tp'), may hold values from -3 to 3
- out_weight: bfloat16 [1152, 1152], P('tp', 'fsdp'), may hold values from -0.75 to 0.75
- out_bias: bfloat16 [1152], replicated, may hold values from -2 to 2
- first_gain: bfloat16 [1152], replicated, may hold values from 0.099609375 to 1.8984375
- first_shift: bfloat16 [1152], replicated, may hold values from -2 to 2
- second_gain: bfloat16 [1152], replicated, may hold values from 0.099609375 to 1.8984375
- second_shift: bfloat16 [1152], replicated, may hold values from -2 to 2
- up_weight: bfloat16 [4304, 1152], P('tp', 'fsdp'), may hold values from -0.1875 to 0.1875
- up_bias: bfloat16 [4304], P('tp'), may hold values from -3 to 3
- down_weight: bfloat16 [4304, 1152], P('tp', 'fsdp'), may hold values from -0.09375 to 0.09375
- down_bias: bfloat16 [1152], replicated, may hold values from -2 to 2
Outputs:
- layer_out: bfloat16 [8, 4, 256, 1152], P('fsdp', 'tp')
- input_grad: float32 [8, 4, 256, 1152], P('fsdp', 'tp')
- joint_grad: float32 [3, 1152, 1152], P(None, 'fsdp', 'tp')
- queryvalue_grad: float32 [2, 1152], replicated
- outweight_grad: float32 [1152, 1152], P('tp', 'fsdp')
- outbias_grad: float32 [1152], replicated
- firstgain_grad: float32 [1152], replicated
- firstshift_grad: float32 [1152], replicated
- secondgain_grad: float32 [1152], replicated
- secondshift_grad: float32 [1152], replicated
- upweight_grad: float32 [4304, 1152], P('tp', 'fsdp')
- upbias_grad: float32 [4304], replicated
- downweight_grad: float32 [4304, 1152], P('tp', 'fsdp')
- downbias_grad: float32 [1152], replicated
Inputs may be any that keep to these rules, and one draw needn't show every extreme that they name: `image_group`: never falling; every group of fsdp holds 1 to 2 images, some group exactly 2; a group's images fill its slots from the first on. `block_sizes`: each row sums to 512; in each row one device's block holds exactly 256 live rows.
All inputs are finite; a program needn't handle non-finite values.
Results may differ from a plain program's by a relative error of at most 0.012.
The roundings to bfloat16 on the way count: a program that leaves them out, or rounds other values in their place, can miss the bound.
Values may be sent and summed in bfloat16 or wider, within the bound.
A program may use at most 128 MiB of HBM per device.

v0:
```python
import math

import jax
import jax.numpy as jnp
from jax import lax
from jax.sharding import PartitionSpec as P

HD = 72
SEQ = 256
SLOTS = 2


EPSILON = 1e-06


def layer_norm(values, scale_row, shift_row):
    center = values - jnp.mean(values, axis=-1, keepdims=True)
    spread = jnp.mean(center * center, axis=-1, keepdims=True)
    return center * lax.rsqrt(spread + EPSILON) * scale_row + shift_row


def gelu_tanh(values):
    return (
        0.5
        * values
        * (1.0 + jnp.tanh(0.7978845608028654 * (values + 0.044715 * values * values * values)))
    )


def contract(former, latter, former_dim, latter_dim):
    return lax.dot_general(
        former,
        latter,
        (((former_dim,), (latter_dim,)), ((), ())),
        preferred_element_type=jnp.float32,
    )


def local(
    hidden_in,
    cotangent,
    image_group,
    block_sizes,
    joint_weight,
    joint_bias,
    out_weight,
    out_bias,
    first_gain,
    first_shift,
    second_gain,
    second_shift,
    up_weight,
    up_bias,
    down_weight,
    down_bias,
):
    split_count = lax.axis_size("tp")
    split_index = lax.axis_index("tp")
    group_index = lax.axis_index("fsdp")
    buffer_rows = hidden_in.shape[2]
    slot_rows = SLOTS * SEQ
    local_width = joint_weight.shape[2]
    local_heads = local_width // HD
    hidden_local = up_weight.shape[0]
    score_scale = 1.0 / math.sqrt(HD)
    block_lengths = block_sizes[0]
    starts = jnp.cumsum(block_lengths) - block_lengths
    block_numbers = jnp.arange(split_count, dtype=jnp.int32)
    slot_index = jnp.arange(slot_rows, dtype=jnp.int32)
    owner_block = jnp.sum((slot_index[:, None] >= starts[None, 1:]).astype(jnp.int32), axis=1)
    owner_start = jnp.sum(
        jnp.where(owner_block[:, None] == block_numbers[None, :], starts[None, :], 0), axis=1
    )
    flat_index = owner_block * buffer_rows + slot_index - owner_start
    padded_index = jnp.arange(split_count * buffer_rows, dtype=jnp.int32)
    padded_offset = padded_index % buffer_rows
    padded_match = (padded_index // buffer_rows)[:, None] == block_numbers[None, :]
    padded_length = jnp.sum(jnp.where(padded_match, block_lengths[None, :], 0), axis=1)
    padded_start = jnp.sum(jnp.where(padded_match, starts[None, :], 0), axis=1)
    padded_used = padded_offset < padded_length
    padded_slot = jnp.where(padded_used, padded_start + padded_offset, 0)
    image_count = jnp.sum((image_group == group_index).astype(jnp.int32))
    padded_live = padded_used & (padded_slot // SEQ < image_count)
    own_live = lax.dynamic_index_in_dim(
        padded_live.reshape(split_count, buffer_rows), split_index, 0, keepdims=False
    )
    live_rows = own_live.astype(jnp.float32)[:, None]

    def to_slots(gathered):
        return jnp.take(gathered, flat_index, axis=0)

    def to_buffers(values):
        return jnp.where(padded_used[:, None], jnp.take(values, padded_slot, axis=0), 0.0)

    def block_sum(slot_terms):
        return lax.psum_scatter(to_buffers(slot_terms), "tp", scatter_dimension=0, tiled=True)

    def split_heads(values):
        return values.reshape(SLOTS, SEQ, local_heads, HD)

    gain_early = first_gain.astype(jnp.float32)
    shift_early = first_shift.astype(jnp.float32)
    gain_late = second_gain.astype(jnp.float32)
    shift_late = second_shift.astype(jnp.float32)
    tokens = hidden_in[0, 0].astype(jnp.float32)
    normed_one = layer_norm(tokens, gain_early, shift_early).astype(jnp.bfloat16)
    joint_full, out_full = (
        lax.all_gather(joint_weight, "fsdp", axis=1, tiled=True),
        lax.all_gather(out_weight, "fsdp", axis=1, tiled=True),
    )
    attention_rows = to_slots(lax.all_gather(normed_one, "tp", axis=0, tiled=True))
    bias_rows = jnp.stack(
        [
            joint_bias[0].astype(jnp.float32),
            jnp.zeros((local_width,), jnp.float32),
            joint_bias[1].astype(jnp.float32),
        ]
    )
    projected = (
        jnp.einsum("rd,cde->cre", attention_rows, joint_full, preferred_element_type=jnp.float32)
        + bias_rows[:, None, :]
    ).astype(jnp.bfloat16)
    query_heads = split_heads(projected[0])
    key_heads = split_heads(projected[1])
    value_heads = split_heads(projected[2])
    scores = (
        jnp.einsum("aqhd,akhd->ahqk", query_heads, key_heads, preferred_element_type=jnp.float32)
        * score_scale
    )
    row_top = jnp.max(scores, axis=-1, keepdims=True)
    log_total = row_top + jnp.log(jnp.sum(jnp.exp(scores - row_top), axis=-1, keepdims=True))
    weights_low = jnp.exp(scores - log_total).astype(jnp.bfloat16)
    mixed_rows = jnp.einsum(
        "ahqk,akhd->aqhd", weights_low, value_heads, preferred_element_type=jnp.float32
    )
    mixed_rows = mixed_rows.reshape(slot_rows, local_width).astype(jnp.bfloat16)
    mixed_sum = block_sum(jnp.dot(mixed_rows, out_full, preferred_element_type=jnp.float32))
    residual = tokens + mixed_sum + out_bias.astype(jnp.float32)
    normed_two = layer_norm(residual, gain_late, shift_late).astype(jnp.bfloat16)
    up_full, down_full = (
        lax.all_gather(up_weight, "fsdp", axis=1, tiled=True),
        lax.all_gather(down_weight, "fsdp", axis=1, tiled=True),
    )
    feed_input = to_slots(lax.all_gather(normed_two, "tp", axis=0, tiled=True))
    preact = contract(feed_input, up_full, 1, 1) + up_bias.astype(jnp.float32)
    activated = gelu_tanh(preact).astype(jnp.bfloat16)
    feed_sum = block_sum(jnp.dot(activated, down_full, preferred_element_type=jnp.float32))
    layer_sum = residual + feed_sum + down_bias.astype(jnp.float32)
    layer_out = (layer_sum * live_rows).astype(jnp.bfloat16)[None, None]
    grad_out = cotangent[0, 0].astype(jnp.float32) * live_rows
    output_rows = to_slots(lax.all_gather(grad_out.astype(jnp.bfloat16), "tp", axis=0, tiled=True))
    grad_act = contract(output_rows, down_full, 1, 1)
    down_grad = contract(activated, output_rows, 0, 0)
    grad_pre = jax.vjp(gelu_tanh, preact)[1](grad_act)[0].astype(jnp.bfloat16)
    up_grad = contract(grad_pre, feed_input, 0, 0)
    upbias_part = jnp.sum(grad_pre.astype(jnp.float32), axis=0)
    up_shard, down_shard = (
        lax.psum_scatter(up_grad, "fsdp", scatter_dimension=1, tiled=True),
        lax.psum_scatter(down_grad, "fsdp", scatter_dimension=1, tiled=True),
    )
    grad_two = block_sum(jnp.dot(grad_pre, up_full, preferred_element_type=jnp.float32))
    late_back = jax.vjp(layer_norm, residual, gain_late, shift_late)[1](grad_two)
    grad_residual = grad_out + late_back[0]
    residual_rows = to_slots(
        lax.all_gather(grad_residual.astype(jnp.bfloat16), "tp", axis=0, tiled=True)
    )
    grad_mixed = contract(residual_rows, out_full, 1, 1).astype(jnp.bfloat16)
    out_grad = contract(mixed_rows, residual_rows, 0, 0)
    grad_heads = split_heads(grad_mixed)
    attention_probs = jnp.exp(
        jnp.einsum("aqhd,akhd->ahqk", query_heads, key_heads, preferred_element_type=jnp.float32)
        * score_scale
        - log_total
    )
    grad_probs = jnp.einsum(
        "aqhd,akhd->ahqk", grad_heads, value_heads, preferred_element_type=jnp.float32
    )
    grad_value = jnp.einsum(
        "ahqk,aqhd->akhd",
        attention_probs.astype(jnp.bfloat16),
        grad_heads,
        preferred_element_type=jnp.float32,
    ).astype(jnp.bfloat16)
    inner_sum = jnp.sum(attention_probs * grad_probs, axis=-1, keepdims=True)
    grad_scores = (attention_probs * (grad_probs - inner_sum)).astype(jnp.bfloat16)
    grad_query = (
        jnp.einsum("ahqk,akhd->aqhd", grad_scores, key_heads, preferred_element_type=jnp.float32)
        * score_scale
    ).astype(jnp.bfloat16)
    grad_key = (
        jnp.einsum("ahqk,aqhd->akhd", grad_scores, query_heads, preferred_element_type=jnp.float32)
        * score_scale
    ).astype(jnp.bfloat16)
    grad_joint = jnp.stack(
        [
            grad_query.reshape(slot_rows, local_width),
            grad_key.reshape(slot_rows, local_width),
            grad_value.reshape(slot_rows, local_width),
        ]
    )
    joint_grad = jnp.einsum(
        "rd,cre->cde", attention_rows, grad_joint, preferred_element_type=jnp.float32
    )
    grad_one = block_sum(
        jnp.einsum("cre,cde->rd", grad_joint, joint_full, preferred_element_type=jnp.float32)
    )
    early_back = jax.vjp(layer_norm, tokens, gain_early, shift_early)[1](grad_one)
    input_grad = (grad_residual + early_back[0])[None, None]
    joint_shard, out_shard = (
        lax.psum_scatter(joint_grad, "fsdp", scatter_dimension=1, tiled=True),
        lax.psum_scatter(out_grad, "fsdp", scatter_dimension=1, tiled=True),
    )
    bias_local = jnp.stack(
        [
            jnp.sum(grad_joint[0].astype(jnp.float32), axis=0),
            jnp.sum(grad_joint[2].astype(jnp.float32), axis=0),
        ]
    )
    bias_whole = lax.dynamic_update_slice_in_dim(
        jnp.zeros((2, local_width * split_count), jnp.float32),
        bias_local,
        split_index * local_width,
        1,
    )
    upbias_whole = lax.dynamic_update_slice_in_dim(
        jnp.zeros((hidden_local * split_count,), jnp.float32),
        upbias_part,
        split_index * hidden_local,
        0,
    )
    small_sums = lax.psum(
        (
            bias_whole,
            jnp.sum(grad_residual, axis=0),
            early_back[1],
            early_back[2],
            late_back[1],
            late_back[2],
            upbias_whole,
            jnp.sum(grad_out, axis=0),
        ),
        ("fsdp", "tp"),
    )
    return (
        layer_out,
        input_grad,
        joint_shard,
        small_sums[0],
        out_shard,
        small_sums[1],
        small_sums[2],
        small_sums[3],
        small_sums[4],
        small_sums[5],
        up_shard,
        small_sums[6],
        down_shard,
        small_sums[7],
    )


def solution(mesh):
    placed = (
        P("fsdp", "tp", None, None),
        P("fsdp", "tp", None, None),
        P(),
        P("fsdp", None),
        P(None, "fsdp", "tp"),
        P(None, "tp"),
        P("tp", "fsdp"),
        P(),
        P(),
        P(),
        P(),
        P(),
        P("tp", "fsdp"),
        P("tp"),
        P("tp", "fsdp"),
        P(),
    )
    return jax.shard_map(
        local,
        mesh=mesh,
        in_specs=placed,
        out_specs=(
            P("fsdp", "tp", None, None),
            P("fsdp", "tp", None, None),
            P(None, "fsdp", "tp"),
            P(),
            P("tp", "fsdp"),
            P(),
            P(),
            P(),
            P(),
            P(),
            P("tp", "fsdp"),
            P(),
            P("tp", "fsdp"),
            P(),
        ),
        check_vma=False,
    )
```

profile of v0, /device:TPU:0, one launch (start us, length us, event | category | flops | bytes accessed | tf_op | source)
XLA Modules:
  0.0 961.9 jit_solution(12869495862722198571)
XLA Ops:
  15.7 34.2 %all_gather.26 = bf16[288,1152]{0,1:T(8,128)(2,1)S(1)} all-gather(bf16[288,144]{0,1:T(8,128)(2,1)S(1)} %copy-done.30), channel_id=1, replica_groups=mesh['fsdp'=8,'tp'=4] {'fsdp'}, dimensions={1}, use_global_device_ids=true | all-gather | bytes 746496 | tf_op jit(solution)/shard_map/all_gather | solution.py:109
  55.3 43.1 %all-gather.10.cloned.1.call-done = bf16[3,1152,288]{2,1,0:T(8,128)(2,1)} async-done(((bf16[3,144,288]{2,1,0:T(8,128)(2,1)}), bf16[3,1152,288]{2,1,0:T(8,128)(2,1)}) %all-gather.10.cloned.1.call-update) | async-done | bytes 1990672 | tf_op jit(solution)/shard_map/all_gather | solution.py:108
  119.0 43.4 %reduce-scatter.11.cloned.1.call-done = f32[256,1152]{1,0:T(8,128)} async-done(((f32[1024,1152]{1,0:T(8,128)}), f32[256,1152]{1,0:T(8,128)}) %reduce-scatter.11.cloned.1.call-update) | async-done | bytes 1179664 | tf_op jit(solution)/shard_map/reduce_scatter | solution.py:96
  167.6 21.0 %all-gather.18.cloned.1.call-done = bf16[1024,1152]{1,0:T(8,128)(2,1)} async-done(((bf16[256,1152]{1,0:T(8,128)(2,1)}), bf16[1024,1152]{1,0:T(8,128)(2,1)}) %all-gather.18.cloned.1.call-update) | async-done | bytes 2359312 | tf_op jit(solution)/shard_map/all_gather | solution.py:151
  193.6 21.2 %all-gather.12.cloned.1.call-done = bf16[1024,1152]{1,0:T(8,128)(2,1)} async-done(((bf16[256,1152]{1,0:T(8,128)(2,1)}), bf16[1024,1152]{1,0:T(8,128)(2,1)}) %all-gather.12.cloned.1.call-update) | async-done | bytes 2359312 | tf_op jit(solution)/shard_map/all_gather | solution.py:144
  219.9 52.2 %all-gather.14.cloned.1.call-done = bf16[1076,1152]{0,1:T(8,128)(2,1)} async-done(((bf16[1076,144]{0,1:T(8,128)(2,1)}), bf16[1076,1152]{0,1:T(8,128)(2,1)}) %all-gather.14.cloned.1.call-update) | async-done | bytes 2479120 | tf_op jit(solution)/shard_map/all_gather | solution.py:141
  277.0 51.1 %all-gather.16.cloned.1.call-done = bf16[1076,1152]{0,1:T(8,128)(2,1)} async-done(((bf16[1076,144]{0,1:T(8,128)(2,1)}), bf16[1076,1152]{0,1:T(8,128)(2,1)}) %all-gather.16.cloned.1.call-update) | async-done | bytes 2479120 | tf_op jit(solution)/shard_map/all_gather | solution.py:142
  328.1 7.1 convert_reduce_fusion
  338.1 5.9 gather_fusion.5
  348.7 6.0 gather_fusion.3
  354.7 7.1 select_select_fusion.1
  362.6 45.8 %reduce-scatter.15.cloned.1.call-done = f32[256,1152]{1,0:T(8,128)} async-done(((f32[1024,1152]{1,0:T(8,128)}), f32[256,1152]{1,0:T(8,128)}) %reduce-scatter.15.cloned.1.call-update) | async-done | bytes 1179664 | tf_op jit(solution)/shard_map/reduce_scatter | solution.py:96
  410.8 48.0 %reduce-scatter.13.cloned.1.call-done = f32[256,1152]{1,0:T(8,128)} async-done(((f32[1024,1152]{1,0:T(8,128)}), f32[256,1152]{1,0:T(8,128)}) %reduce-scatter.13.cloned.1.call-update) | async-done | bytes 1179664 | tf_op jit(solution)/shard_map/reduce_scatter | solution.py:96
  463.6 24.2 %all-gather.20.cloned.1.call-done = bf16[1024,1152]{1,0:T(8,128)(2,1)} async-done(((bf16[256,1152]{1,0:T(8,128)(2,1)}), bf16[1024,1152]{1,0:T(8,128)(2,1)}) %all-gather.20.cloned.1.call-update) | async-done | bytes 2359312 | tf_op jit(solution)/shard_map/all_gather | solution.py:165
  511.5 8.6 copy.98
  520.0 8.9 reshape.272
  533.3 5.7 gather_fusion.7
  544.8 5.9 fusion.35
  560.4 56.4 %reduce-scatter.25.cloned.1.call-done = f32[144,864]{1,0:T(8,128)} async-done(((f32[1152,864]{1,0:T(8,128)}), f32[144,864]{1,0:T(8,128)}) %reduce-scatter.25.cloned.1.call-update) | async-done | bytes 497680
  619.4 47.5 %reduce-scatter.17.cloned.1.call-done = f32[256,1152]{1,0:T(8,128)} async-done(((f32[1024,1152]{1,0:T(8,128)}), f32[256,1152]{1,0:T(8,128)}) %reduce-scatter.17.cloned.1.call-update) | async-done | bytes 1179664 | tf_op jit(solution)/shard_map/reduce_scatter | solution.py:96
  672.2 44.8 %all-reduce = (f32[2,1152]{1,0:T(2,128)}, f32[1152]{0:T(1024)}, f32[1152]{0:T(1024)}, f32[1152]{0:T(1024)}, f32[1152]{0:T(1024)}, /*index=5*/f32[1152]{0:T(1024)}, f32[4304]{0:T(1024)}, f32[1152]{0:T(1024)}) all-reduce(f32[2,1152]{1,0:T(2,128)S(1)} %dynamic_update_slice.6, ...), channel_id=1, replica_groups=mesh['fsdp'=8,'tp'=4] {'fsdp','tp'}, use_global_device_ids=true, to_apply=%region_24.27 | all-reduce | flops 13520 | bytes 108160 | tf_op jit(solution)/shard_map/psum | solution.py:231
  717.0 59.8 %reduce-scatter.23.cloned.1.call-done = f32[1076,144]{0,1:T(8,128)} async-done(((f32[1076,1152]{0,1:T(8,128)}), f32[1076,144]{0,1:T(8,128)}) %reduce-scatter.23.cloned.1.call-update) | async-done | bytes 619792 | tf_op jit(solution)/shard_map/reduce_scatter | solution.py:159
  776.8 108.0 %reduce-scatter.21.cloned.1.call-done = f32[1076,144]{0,1:T(8,128)} async-done(((f32[1076,1152]{0,1:T(8,128)}), f32[1076,144]{0,1:T(8,128)}) %reduce-scatter.21.cloned.1.call-update) | async-done | bytes 619792 | tf_op jit(solution)/shard_map/reduce_scatter | solution.py:158
  884.8 70.1 %reduce-scatter.19.cloned.1.call-done = f32[288,144]{0,1:T(8,128)} async-done(((f32[288,1152]{0,1:T(8,128)}), f32[288,144]{0,1:T(8,128)}) %reduce-scatter.19.cloned.1.call-update) | async-done | bytes 165904 | tf_op jit(solution)/shard_map/reduce_scatter | solution.py:211
  (284 shorter events, 120.5 us)
Async XLA Ops:
  7.2 42.7 %all-gather.8.cloned.1.call-start = ((), (), s32[]{:S(2)}) async-start(), calls=%async_computation.8 | async-start | bytes 2949120 | tf_op jit(solution)/shard_map/all_gather | solution.py:111
  14.0 84.3 %all-gather.10.cloned.1.call-start = ((), (), s32[]{:S(2)}) async-start(), calls=%async_computation.9 | async-start | bytes 2985984 | tf_op jit(solution)/shard_map/all_gather | solution.py:108
  14.8 147.7 %reduce-scatter.11.cloned.1.call-start = ((), (), s32[]{:S(2)}) async-start(), calls=%async_computation.10 | async-start | bytes 5898240 | tf_op jit(solution)/shard_map/reduce_scatter | solution.py:96
  15.3 83.0 %copy-start.62 = (pred[512]{0:T(512)(128)(4,1)}, pred[512]{0:T(512)(128)(4,1)S(1)}, u32[]{:S(2)}) copy-start(pred[512]{0:T(512)(128)(4,1)S(1)} %get-tuple-element.100) | copy-start | bytes 1540
  15.6 95.9 %copy-start.42 = (pred[1024]{0:T(1024)(128)(4,1)}, pred[1024]{0:T(1024)(128)(4,1)S(1)}, u32[]{:S(2)}) copy-start(pred[1024]{0:T(1024)(128)(4,1)S(1)} %get-tuple-element.99) | copy-start | bytes 3076
  15.6 95.9 %copy-start.51 = (pred[1024]{0:T(1024)(128)(4,1)}, pred[1024]{0:T(1024)(128)(4,1)S(1)}, u32[]{:S(2)}) copy-start(pred[1024]{0:T(1024)(128)(4,1)S(1)} %get-tuple-element.98) | copy-start | bytes 3076
  15.6 90.2 %copy-start.31 = (s32[1024]{0:T(1024)}, s32[1024]{0:T(1024)S(1)}, u32[]{:S(2)}) copy-start(s32[1024]{0:T(1024)S(1)} %broadcast_clamp_fusion) | copy-start | bytes 12292
  115.9 72.7 %all-gather.18.cloned.1.call-start = ((), (), s32[]{:S(2)}) async-start(), calls=%async_computation.15 | async-start | bytes 2949120 | tf_op jit(solution)/shard_map/all_gather | solution.py:151
  118.9 95.9 %all-gather.12.cloned.1.call-start = ((), (), s32[]{:S(2)}) async-start(), calls=%async_computation.11 | async-start | bytes 2949120 | tf_op jit(solution)/shard_map/all_gather | solution.py:144
  165.4 106.7 %all-gather.14.cloned.1.call-start = ((), (), s32[]{:S(2)}) async-start(), calls=%async_computation.12 | async-start | bytes 2985984 | tf_op jit(solution)/shard_map/all_gather | solution.py:141
  166.0 162.1 %all-gather.16.cloned.1.call-start = ((), (), s32[]{:S(2)}) async-start(), calls=%async_computation.13 | async-start | bytes 2985984 | tf_op jit(solution)/shard_map/all_gather | solution.py:142
  166.8 241.6 %reduce-scatter.15.cloned.1.call-start = ((), (), s32[]{:S(2)}) async-start(), calls=%async_computation.16 | async-start | bytes 5898240 | tf_op jit(solution)/shard_map/reduce_scatter | solution.py:96
  193.6 134.6 %copy-start.26 = (bf16[512,1152]{1,0:T(8,128)(2,1)}, bf16[512,1152]{1,0:T(8,128)(2,1)S(1)}, u32[]{:S(2)}) copy-start(bf16[512,1152]{1,0:T(8,128)(2,1)S(1)} %gather_fusion.4) | copy-start | bytes 3538948
  219.8 57.1 %copy-start.24 = (bf16[512,1152]{1,0:T(8,128)(2,1)}, bf16[512,1152]{1,0:T(8,128)(2,1)S(1)}, u32[]{:S(2)}) copy-start(bf16[512,1152]{1,0:T(8,128)(2,1)S(1)} %gather_fusion.2) | copy-start | bytes 3538948
  361.8 97.0 %reduce-scatter.13.cloned.1.call-start = ((), (), s32[]{:S(2)}) async-start(), calls=%async_computation.14 | async-start | bytes 5898240 | tf_op jit(solution)/shard_map/reduce_scatter | solution.py:96
  362.5 96.3 %copy-start.45 = (f32[1,256]{1,0:T(1,128)S(1)}, f32[1,256]{1,0:T(1,128)}, u32[]{:S(2)}) copy-start(f32[1,256]{1,0:T(1,128)} %copy-done.44) | copy-start | bytes 3076
  362.5 125.2 %all-gather.20.cloned.1.call-start = ((), (), s32[]{:S(2)}) async-start(), calls=%async_computation.17 | async-start | bytes 2949120 | tf_op jit(solution)/shard_map/all_gather | solution.py:165
  463.5 153.3 %reduce-scatter.25.cloned.1.call-start = ((), (), s32[]{:S(2)}) async-start(), calls=%async_computation.22 | async-start | bytes 4644864
  529.0 137.8 %reduce-scatter.17.cloned.1.call-start = ((), (), s32[]{:S(2)}) async-start(), calls=%async_computation.18 | async-start | bytes 5898240 | tf_op jit(solution)/shard_map/reduce_scatter | solution.py:96
  543.5 233.2 %reduce-scatter.23.cloned.1.call-start = ((), (), s32[]{:S(2)}) async-start(), calls=%async_computation.21 | async-start | bytes 5971968 | tf_op jit(solution)/shard_map/reduce_scatter | solution.py:159
  550.7 334.1 %reduce-scatter.21.cloned.1.call-start = ((), (), s32[]{:S(2)}) async-start(), calls=%async_computation.20 | async-start | bytes 5971968 | tf_op jit(solution)/shard_map/reduce_scatter | solution.py:158
  556.6 398.3 %reduce-scatter.19.cloned.1.call-start = ((), (), s32[]{:S(2)}) async-start(), calls=%async_computation.19 | async-start | bytes 1990656 | tf_op jit(solution)/shard_map/reduce_scatter | solution.py:211
  559.7 107.1 %copy-start.3 = (bf16[1,1,256,1152]{3,2,1,0:T(8,128)(2,1)S(1)}, bf16[1,1,256,1152]{3,2,1,0:T(8,128)(2,1)}, u32[]{:S(2)}) copy-start(bf16[1,1,256,1152]{3,2,1,0:T(8,128)(2,1)} %param.20) | copy-start | bytes 1769476
  559.7 107.1 %copy-start.34 = (f32[256]{0:T(256)S(1)}, f32[256]{0:T(256)}, u32[]{:S(2)}) copy-start(f32[256]{0:T(256)} %copy-done.33) | copy-start | bytes 3076
  (67 other events, 1162.9 us)
Sparse Core Ops, SparseCore 0:
  14.1 26.8 all-gather.7
  43.2 55.0 all-gather.9
  116.0 46.3 reduce-scatter.10
  164.5 24.0 all-gather.17
  190.7 24.0 all-gather.11
  217.0 55.0 all-gather.13
  274.5 53.5 all-gather.15
  361.9 46.4 reduce-scatter.14
  410.9 47.8 reduce-scatter.12
  463.6 24.0 all-gather.19
  529.1 87.6 reduce-scatter.24
  619.2 47.5 reduce-scatter.16
  671.4 105.2 reduce-scatter.22
  780.8 103.9 reduce-scatter.20
  889.1 65.7 reduce-scatter.18
where the time goes:
time: 970 us; the launch traced here: 962 us
  waiting for transfers between devices  695 us (72%)
  local copies, waits for them, and re-layouts  80.8 us (8%)
  blocking collectives  79 us (8%)
  matrix products  50.4 us (5%)
  other arithmetic  40.6 us (4%)
  between operations  15.4 us (2%)
    reduce_scatter x4, waiting for transfers between devices, block_sum(): lax.psum_scatter(to_buffers(slot_terms), 'tp', scatter_dimension=0, tiled...  185 us
    reduce_scatter x1, waiting for transfers between devices, local(): lax.psum_scatter(up_grad, 'fsdp', scatter_dimension=1, tiled=True)  108 us
    reduce_scatter x1, waiting for transfers between devices, local(): lax.psum_scatter(out_grad, 'fsdp', scatter_dimension=1, tiled=True)  70.1 us
    reduce_scatter x1, waiting for transfers between devices, local(): lax.psum_scatter(down_grad, 'fsdp', scatter_dimension=1, tiled=True)  59.8 us
    unnamed x16, waiting for transfers between devices  59.1 us
    all_gather x1, waiting for transfers between devices, local(): lax.all_gather(up_weight, 'fsdp', axis=1, tiled=True)  52.2 us
    all_gather x1, waiting for transfers between devices, local(): lax.all_gather(down_weight, 'fsdp', axis=1, tiled=True)  51.1 us
    psum x1, blocking collectives, local(): lax.psum((bias_whole, jnp.sum(grad_residual, axis=0), early_back[1], earl...  44.8 us
  transfers between devices with their start and end apart: 15, of which 14 were waited for; matrix products, arithmetic and copies ran while one was open for 7% of the time, Pallas kernels for 0%

commit v1 on v0

v1 whole, which is shorter than its diff:
```python
import math

import jax
import jax.numpy as jnp
from jax import lax
from jax.sharding import PartitionSpec as P

HD = 72
SEQ = 256
SLOTS = 2


EPSILON = 1e-06


def layer_norm(values, scale_row, shift_row):
    center = values - jnp.mean(values, axis=-1, keepdims=True)
    spread = jnp.mean(center * center, axis=-1, keepdims=True)
    return center * lax.rsqrt(spread + EPSILON) * scale_row + shift_row


def gelu_tanh(values):
    return (
        0.5
        * values
        * (1.0 + jnp.tanh(0.7978845608028654 * (values + 0.044715 * values * values * values)))
    )


def contract(former, latter, former_dim, latter_dim):
    return lax.dot_general(
        former,
        latter,
        (((former_dim,), (latter_dim,)), ((), ())),
        preferred_element_type=jnp.float32,
    )


def local(
    hidden_in,
    cotangent,
    image_group,
    block_sizes,
    joint_weight,
    joint_bias,
    out_weight,
    out_bias,
    first_gain,
    first_shift,
    second_gain,
    second_shift,
    up_weight,
    up_bias,
    down_weight,
    down_bias,
):
    split_count = lax.axis_size("tp")
    split_index = lax.axis_index("tp")
    group_index = lax.axis_index("fsdp")
    buffer_rows = hidden_in.shape[2]
    width = hidden_in.shape[3]
    slot_rows = SLOTS * SEQ
    local_width = joint_weight.shape[2]
    local_heads = local_width // HD
    hidden_local = up_weight.shape[0]
    score_scale = 1.0 / math.sqrt(HD)
    half = slot_rows // 2
    core = split_index % 2
    low = jnp.bfloat16
    f32 = jnp.float32
    sibling = [(i, i ^ 1) for i in range(split_count)]
    across = [(i, i ^ 2) for i in range(split_count)]

    groups = lax.axis_size("fsdp")
    ringed = groups == 8
    ring = list(range(groups))
    if ringed:
        ring = ring[0::2] + ring[1::2][::-1]
    forth = [(ring[i], ring[(i + 1) % groups]) for i in range(groups)]
    back = [(b, a) for a, b in forth]
    depth = joint_weight.shape[1]
    cut = (depth // 32) * 16
    places = jnp.array(ring, jnp.int32)
    position = jnp.sum(jnp.where(places == group_index, jnp.arange(groups), 0))
    feature = jnp.arange(width, dtype=jnp.int32)
    near_index = (position + feature // depth) % groups
    if not ringed:
        near_index = feature // depth
    owner = jnp.sum(
        jnp.where(near_index[:, None] == jnp.arange(groups)[None, :], places[None, :], 0), axis=1
    )
    source = owner * depth + feature % depth
    turn = (feature[:, None] == source[None, :]).astype(low)

    def ring_gather(shard):
        if not ringed:
            return lax.all_gather(shard, "fsdp", axis=0, tiled=True)
        ahead, behind = [], []
        first = second = shard
        for _ in range(groups // 2 - 1):
            first = lax.ppermute(first, "fsdp", forth)
            second = lax.ppermute(second, "fsdp", back)
            behind.append(first)
            ahead.append(second)
        top = lax.ppermute(first[:cut], "fsdp", forth)
        bottom = lax.ppermute(second[cut:], "fsdp", back)
        mixed = jnp.concatenate([shard, *ahead, top, bottom, *behind[::-1]], axis=0)
        return jnp.dot(turn, mixed, preferred_element_type=f32).astype(low)

    def ring_order(values):
        if not ringed:
            return values
        return jnp.dot(values, turn, preferred_element_type=f32).astype(low)

    def ring_scatter(terms):
        if not ringed:
            return lax.psum_scatter(
                terms.astype(low), "fsdp", scatter_dimension=0, tiled=True
            ).astype(f32)
        middle = groups // 2

        def chunk(number):
            return terms[number * depth : (number + 1) * depth]

        far = chunk(middle).astype(low)
        top = lax.ppermute(far[:cut], "fsdp", forth).astype(f32)
        bottom = lax.ppermute(far[cut:], "fsdp", back).astype(f32)
        held = chunk(middle - 1)
        first = jnp.concatenate([held[:cut] + top, held[cut:]], axis=0)
        held = chunk(middle + 1)
        second = jnp.concatenate([held[:cut], held[cut:] + bottom], axis=0)
        for step in range(1, middle):
            first = lax.ppermute(first.astype(low), "fsdp", forth).astype(f32)
            second = lax.ppermute(second.astype(low), "fsdp", back).astype(f32)
            if step < middle - 1:
                first = first + chunk(middle - 1 - step)
                second = second + chunk(middle + 1 + step)
        return chunk(0) + first + second

    def sum_everywhere(values):
        for axis in ("tp", "fsdp"):
            size, bit = lax.axis_size(axis), 1
            while bit < size:
                pairs = [(i, i ^ bit) for i in range(size)]
                values = values + lax.ppermute(values, axis, pairs)
                bit *= 2
        return values

    def join(mine, other, side):
        first = side == 0
        return jnp.concatenate([jnp.where(first, mine, other), jnp.where(first, other, mine)], 0)

    def gather_blocks(block):
        far = lax.ppermute(block, "tp", across)
        pair = join(block, far, split_index // 2)
        other = lax.ppermute(pair, "tp", sibling)
        mine = pair.reshape(2, buffer_rows, width)
        theirs = other.reshape(2, buffer_rows, width)
        first = core == 0
        return jnp.stack(
            [jnp.where(first, mine, theirs), jnp.where(first, theirs, mine)], 1
        ).reshape(split_count * buffer_rows, width)

    def sum_slots(partial):
        kept = lax.dynamic_slice_in_dim(partial, core * half, half, 0)
        given = lax.dynamic_slice_in_dim(partial, (1 - core) * half, half, 0)
        near = lax.ppermute(given.astype(low), "tp", sibling)
        chip = (kept + near.astype(f32)).astype(low)
        far = lax.ppermute(chip, "tp", across)
        whole = (chip.astype(f32) + far.astype(f32)).astype(low)
        other = lax.ppermute(whole, "tp", sibling)
        return join(whole, other, core)

    block_lengths = block_sizes[0]
    starts = jnp.cumsum(block_lengths) - block_lengths
    block_numbers = jnp.arange(split_count, dtype=jnp.int32)
    slot_index = jnp.arange(slot_rows, dtype=jnp.int32)
    owner_block = jnp.sum((slot_index[:, None] >= starts[None, 1:]).astype(jnp.int32), axis=1)
    owner_start = jnp.sum(
        jnp.where(owner_block[:, None] == block_numbers[None, :], starts[None, :], 0), axis=1
    )
    flat_index = owner_block * buffer_rows + slot_index - owner_start
    place = (
        flat_index[:, None] == jnp.arange(split_count * buffer_rows, dtype=jnp.int32)[None, :]
    ).astype(low)
    image_count = jnp.sum((image_group == group_index).astype(jnp.int32))
    live = (slot_index // SEQ < image_count).astype(f32)[:, None]
    own_start = jnp.sum(jnp.where(block_numbers == split_index, starts, 0))
    own_length = jnp.sum(jnp.where(block_numbers == split_index, block_lengths, 0))
    offsets = jnp.arange(buffer_rows, dtype=jnp.int32)
    own_used = offsets < own_length
    own_slot = own_start + offsets
    pick = ((own_slot[:, None] == slot_index[None, :]) & own_used[:, None]).astype(low)
    own_live = (own_used & (own_slot // SEQ < image_count)).astype(f32)[:, None]

    def to_slots(gathered):
        return jnp.dot(place, gathered, preferred_element_type=f32)

    def own_rows(values):
        return jnp.dot(pick, values, preferred_element_type=f32)

    def split_heads(values):
        return values.reshape(SLOTS, SEQ, local_heads, HD)

    gain_early = first_gain.astype(f32)
    shift_early = first_shift.astype(f32)
    gain_late = second_gain.astype(f32)
    shift_late = second_shift.astype(f32)
    attention_shard = jnp.concatenate(
        [joint_weight[0], joint_weight[1], joint_weight[2], out_weight.T], axis=1
    )
    attention_full = ring_gather(attention_shard)
    up_full = lax.all_gather(up_weight.T, "fsdp", axis=0, tiled=True)
    down_full = lax.all_gather(down_weight.T, "fsdp", axis=0, tiled=True)
    joint_full = attention_full[:, : 3 * local_width]
    out_full = attention_full[:, 3 * local_width :]

    tokens = to_slots(gather_blocks(hidden_in[0, 0]))
    attention_rows = layer_norm(tokens, gain_early, shift_early).astype(low)
    bias_row = jnp.concatenate(
        [
            joint_bias[0].astype(f32),
            jnp.zeros((local_width,), f32),
            joint_bias[1].astype(f32),
        ]
    )
    projected = (jnp.dot(attention_rows, joint_full, preferred_element_type=f32) + bias_row).astype(
        low
    )
    query_heads = split_heads(projected[:, :local_width])
    key_heads = split_heads(projected[:, local_width : 2 * local_width])
    value_heads = split_heads(projected[:, 2 * local_width :])
    scores = (
        jnp.einsum("aqhd,akhd->ahqk", query_heads, key_heads, preferred_element_type=f32)
        * score_scale
    )
    raised = jnp.exp(scores - jnp.max(scores, axis=-1, keepdims=True))
    probs = raised * (1.0 / jnp.sum(raised, axis=-1, keepdims=True))
    weights_low = probs.astype(low)
    mixed_rows = jnp.einsum("ahqk,akhd->aqhd", weights_low, value_heads, preferred_element_type=f32)
    mixed_rows = mixed_rows.reshape(slot_rows, local_width).astype(low)
    mixed_sum = sum_slots(contract(mixed_rows, out_full, 1, 1))
    out_shift = out_bias.astype(f32)
    residual = tokens + mixed_sum.astype(f32) + out_shift
    feed_input = layer_norm(residual, gain_late, shift_late).astype(low)

    output_rows = to_slots(gather_blocks(cotangent[0, 0])) * live
    output_low = output_rows.astype(low)

    preact = jnp.dot(feed_input, up_full, preferred_element_type=f32) + up_bias.astype(f32)
    activated = gelu_tanh(preact).astype(low)
    grad_act = jnp.dot(output_low, down_full, preferred_element_type=f32)
    grad_pre = jax.vjp(gelu_tanh, preact)[1](grad_act)[0].astype(low)
    grad_two = sum_slots(contract(grad_pre, up_full, 1, 1)).astype(f32)
    down_grad = contract(output_low, activated, 0, 0).astype(low)
    down_shard = lax.psum_scatter(down_grad, "fsdp", scatter_dimension=0, tiled=True)
    up_grad = contract(feed_input, grad_pre, 0, 0).astype(low)
    up_shard = lax.psum_scatter(up_grad, "fsdp", scatter_dimension=0, tiled=True)
    feed_sum = sum_slots(contract(activated, down_full, 1, 1))
    own_residual = hidden_in[0, 0].astype(f32) + own_rows(mixed_sum) + out_shift
    layer_sum = own_residual + own_rows(feed_sum) + down_bias.astype(f32)
    layer_out = (layer_sum * own_live).astype(low)[None, None]

    late_back = jax.vjp(layer_norm, residual, gain_late, shift_late)[1](grad_two)
    grad_residual = output_rows + late_back[0]
    residual_low = grad_residual.astype(low)
    grad_mixed = jnp.dot(residual_low, out_full, preferred_element_type=f32).astype(low)
    out_grad = contract(ring_order(residual_low), mixed_rows, 0, 0)
    grad_heads = split_heads(grad_mixed)
    grad_probs = jnp.einsum("aqhd,akhd->ahqk", grad_heads, value_heads, preferred_element_type=f32)
    grad_value = jnp.einsum(
        "ahqk,aqhd->akhd", weights_low, grad_heads, preferred_element_type=f32
    ).astype(low)
    inner_sum = jnp.sum(probs * grad_probs, axis=-1, keepdims=True)
    grad_scores = (probs * (grad_probs - inner_sum)).astype(low)
    grad_query = (
        jnp.einsum("ahqk,akhd->aqhd", grad_scores, key_heads, preferred_element_type=f32)
        * score_scale
    ).astype(low)
    grad_key = (
        jnp.einsum("ahqk,aqhd->akhd", grad_scores, query_heads, preferred_element_type=f32)
        * score_scale
    ).astype(low)
    grad_joint = jnp.concatenate(
        [
            grad_query.reshape(slot_rows, local_width),
            grad_key.reshape(slot_rows, local_width),
            grad_value.reshape(slot_rows, local_width),
        ],
        axis=1,
    )
    grad_one = sum_slots(contract(grad_joint, joint_full, 1, 1))
    joint_grad = contract(ring_order(attention_rows), grad_joint, 0, 0)
    attention_grad = jnp.concatenate([joint_grad, out_grad], axis=1)
    attention_part = ring_scatter(attention_grad)
    residual_rest = (grad_residual - residual_low.astype(f32)).astype(low)
    own_grad = own_rows(residual_low) + own_rows(residual_rest)
    early_back = jax.vjp(layer_norm, hidden_in[0, 0].astype(f32), gain_early, shift_early)[1](
        own_rows(grad_one)
    )
    input_grad = (own_grad + early_back[0])[None, None]
    joint_shard = jnp.stack(
        [attention_part[:, i * local_width : (i + 1) * local_width] for i in range(3)]
    )
    out_shard = attention_part[:, 3 * local_width :].T

    def one_of(values):
        return jnp.where(split_index == 0, values, 0.0)

    joint_sums = jnp.sum(grad_joint.astype(f32), axis=0)
    bias_whole = lax.dynamic_update_slice_in_dim(
        jnp.zeros((2, local_width * split_count), f32),
        jnp.stack([joint_sums[:local_width], joint_sums[2 * local_width :]]),
        split_index * local_width,
        1,
    )
    upbias_whole = lax.dynamic_update_slice_in_dim(
        jnp.zeros((hidden_local * split_count,), f32),
        jnp.sum(grad_pre.astype(f32), axis=0),
        split_index * hidden_local,
        0,
    )
    pieces = [
        bias_whole.reshape(-1),
        one_of(jnp.sum(grad_residual, axis=0)),
        early_back[1],
        early_back[2],
        one_of(late_back[1]),
        one_of(late_back[2]),
        upbias_whole,
        one_of(jnp.sum(output_rows, axis=0)),
    ]
    summed = sum_everywhere(jnp.concatenate(pieces))
    small_sums, at = [], 0
    for piece in pieces:
        small_sums.append(lax.slice_in_dim(summed, at, at + piece.shape[0]))
        at += piece.shape[0]
    return (
        layer_out,
        input_grad,
        joint_shard,
        small_sums[0].reshape(2, width),
        out_shard,
        small_sums[1],
        small_sums[2],
        small_sums[3],
        small_sums[4],
        small_sums[5],
        up_shard.astype(f32).T,
        small_sums[6],
        down_shard.astype(f32).T,
        small_sums[7],
    )


def solution(mesh):
    placed = (
        P("fsdp", "tp", None, None),
        P("fsdp", "tp", None, None),
        P(),
        P("fsdp", None),
        P(None, "fsdp", "tp"),
        P(None, "tp"),
        P("tp", "fsdp"),
        P(),
        P(),
        P(),
        P(),
        P(),
        P("tp", "fsdp"),
        P("tp"),
        P("tp", "fsdp"),
        P(),
    )
    return jax.shard_map(
        local,
        mesh=mesh,
        in_specs=placed,
        out_specs=(
            P("fsdp", "tp", None, None),
            P("fsdp", "tp", None, None),
            P(None, "fsdp", "tp"),
            P(),
            P("tp", "fsdp"),
            P(),
            P(),
            P(),
            P(),
            P(),
            P("tp", "fsdp"),
            P(),
            P("tp", "fsdp"),
            P(),
        ),
        check_vma=False,
    )
```

time: 970 us -> 352 us (0.36)
  waiting for transfers between devices: 695 us -> 145 us
  blocking collectives: 79 us -> 0 us
  local copies, waits for them, and re-layouts: 80.8 us -> 25.3 us
  starting transfers between devices: 1.03 us -> 37.9 us
  matrix products: 50.4 us -> 72.7 us
  other arithmetic: 40.6 us -> 50.9 us
    reduce_scatter x7 -> x2, waiting for transfers between devices: 423 us -> 0.01 us  [the longest x1 0.01 us: local(): lax.psum_scatter(up_grad, 'fsdp', scatter_dimension=0, tiled=True)]
    all_gather x7 -> x2, waiting for transfers between devices: 213 us -> 19.4 us  [the longest x1 19.4 us: local(): down_full = lax.all_gather(down_weight.T, 'fsdp', axis=0, tiled=True)]
    ppermute x0 -> x37, waiting for transfers between devices: none -> 126 us  [the longest x4 30 us: sum_slots(): far = lax.ppermute(chip, 'tp', across)]
    unnamed x16 -> x4, waiting for transfers between devices: 59.1 us -> 0.07 us
    psum x1 -> x0, blocking collectives: 44.8 us -> none  [local(): lax.psum((bias_whole, jnp.sum(grad_residual, axis=0), early_back[1], earl...]
    gather x8 -> x0, local copies, waits for them, and re-layouts: 43.6 us -> none  [the longest x4 23.3 us: to_buffers(): jnp.take(values, padded_slot, axis=0)]
    ppermute x0 -> x37, starting transfers between devices: none -> 37 us  [the longest x3 10 us: ring_scatter(): first = lax.ppermute(first.astype(low), 'fsdp', forth).astype(f32)]
    all_gather x1 -> x0, blocking collectives: 34.2 us -> none  [local(): lax.all_gather(out_weight, 'fsdp', axis=1, tiled=True)]
  transfers between devices with their start and end apart: 15 -> 41, of which waited for: 14 -> 18; matrix products, arithmetic and copies ran while one was open for 7% -> 36% of each run, Pallas kernels for 0% -> 0%
where the time goes in v1:
time: 352 us; the launch traced here: 347 us
  waiting for transfers between devices  145 us (41%)
  matrix products  72.7 us (21%)
  other arithmetic  50.9 us (14%)
  starting transfers between devices  37.9 us (11%)
  local copies, waits for them, and re-layouts  25.3 us (7%)
  between operations  15.4 us (4%)
    ppermute x4, waiting for transfers between devices, sum_slots(): far = lax.ppermute(chip, 'tp', across)  30 us
    dot_general x8, matrix products, contract(): lax.dot_general(former, latter, (((former_dim,), (latter_dim,)), ((), ())...  29.5 us
    ppermute x3, waiting for transfers between devices, ring_scatter(): first = lax.ppermute(first.astype(low), 'fsdp', forth).astype(f32)  20.4 us
    all_gather x1, waiting for transfers between devices, local(): down_full = lax.all_gather(down_weight.T, 'fsdp', axis=0, tiled=True)  19.4 us
    ppermute x3, waiting for transfers between devices, ring_scatter(): second = lax.ppermute(second.astype(low), 'fsdp', back).astype(f32)  16.7 us
    ppermute x2, waiting for transfers between devices, gather_blocks(): far = lax.ppermute(block, 'tp', across)  14.9 us
    ppermute x5, waiting for transfers between devices, sum_everywhere(): values = values + lax.ppermute(values, axis, pairs)  13.9 us
    ppermute x1, waiting for transfers between devices, ring_gather(): bottom = lax.ppermute(second[cut:], 'fsdp', back)  13.6 us
  transfers between devices with their start and end apart: 41, of which 18 were waited for; matrix products, arithmetic and copies ran while one was open for 36% of the time, Pallas kernels for 0%

profile of v1, /device:TPU:0, one launch (start us, length us, event | category | flops | bytes accessed | tf_op | source)
XLA Modules:
  0.0 347.2 jit_solution(17014130784329300233)
XLA Ops:
  25.0 4.1 %collective-permute-done = bf16[256,1152]{1,0:T(8,128)(2,1)S(1)} collective-permute-done((bf16[256,1152]{1,0:T(8,128)(2,1)}, bf16[256,1152]{1,0:T(8,128)(2,1)S(1)}, u32[]{:S(2)}, u32[]{:S(2)}) %collective-permute-start) | collective-permute-done | bytes 589856 | tf_op jit(solution)/shard_map/ppermute | solution.py:154
  29.4 10.8 %collective-permute-done.16 = bf16[256,1152]{1,0:T(8,128)(2,1)S(1)} collective-permute-done((bf16[256,1152]{1,0:T(8,128)(2,1)}, bf16[256,1152]{1,0:T(8,128)(2,1)S(1)}, u32[]{:S(2)}, u32[]{:S(2)}) %collective-permute-start.16) | collective-permute-done | bytes 589856 | tf_op jit(solution)/shard_map/ppermute | solution.py:154
  44.2 7.2 %collective-permute-done.7 = bf16[144,1152]{1,0:T(8,128)(2,1)S(1)} collective-permute-done((bf16[144,1152]{1,0:T(8,128)(2,1)S(1)}, bf16[144,1152]{1,0:T(8,128)(2,1)S(1)}, u32[]{:S(2)}, u32[]{:S(2)}) %collective-permute-start.7) | collective-permute-done | bytes 331808 | tf_op jit(solution)/shard_map/ppermute | solution.py:101
  53.9 6.3 %collective-permute-done.8 = bf16[64,1152]{1,0:T(8,128)(2,1)S(1)} collective-permute-done((bf16[64,1152]{1,0:T(8,128)(2,1)S(1)}, bf16[64,1152]{1,0:T(8,128)(2,1)S(1)}, u32[]{:S(2)}, u32[]{:S(2)}) %collective-permute-start.8) | collective-permute-done | bytes 147488 | tf_op jit(solution)/shard_map/ppermute | solution.py:105
  60.2 13.6 %collective-permute-done.9 = bf16[80,1152]{1,0:T(8,128)(2,1)S(1)} collective-permute-done((bf16[80,1152]{1,0:T(8,128)(2,1)S(1)}, bf16[80,1152]{1,0:T(8,128)(2,1)S(1)}, u32[]{:S(2)}, u32[]{:S(2)}) %collective-permute-start.9) | collective-permute-done | bytes 184352 | tf_op jit(solution)/shard_map/ppermute | solution.py:106
  74.0 4.1 %convolution_convert_fusion.2 = bf16[1152,1152]{0,1:T(8,128)(2,1)S(1)} fusion(bf16[1152,1152]{1,0:T(8,128)(2,1)S(1)} %constant_dynamic-update-slice_fusion, s32[1152]{0:T(1024)S(1)} %fusion.140), kind=kOutput, calls=%fused_computation.11 | convolution fusion | flops 3060301824 | bytes 5313024 | tf_op jit(solution)/shard_map/dot_general | solution.py:108
  104.2 12.2 %collective-permute-done.11 = bf16[256,1152]{1,0:T(8,128)(2,1)S(1)} collective-permute-done((bf16[256,1152]{1,0:T(8,128)(2,1)S(1)}, bf16[256,1152]{1,0:T(8,128)(2,1)S(1)}, u32[]{:S(2)}, u32[]{:S(2)}) %collective-permute-start.11) | collective-permute-done | bytes 589856 | tf_op jit(solution)/shard_map/ppermute | solution.py:169
  124.8 5.0 %convolution_add_fusion = f32[512,1076]{0,1:T(8,128)} fusion(bf16[1152,1076]{1,0:T(8,128)(2,1)} %all-gather.3.cloned.1.call-done, f32[1076]{0:T(1024)} %convert_element_type.292, f32[512,1152]{1,0:T(8,128)S(1)} %get-tuple-element.83, f32[1152]{0:T(1024)} %convert_element_type.290, f32[1152]{0:T(1024)S(1)} %convert_element_type.289, f32[512]{0:T(512)} %fusion.147, ...), kind=kOutput, calls=%fused_computation.28 | convolution fusion | flops 1272801280 | bytes 7059664 | tf_op jit(solution)/shard_map/dot_general | solution.py:250
  129.7 19.4 %all-gather.5.cloned.1.call-done = bf16[1152,1076]{1,0:T(8,128)(2,1)} async-done(((bf16[144,1076]{1,0:T(8,128)(2,1)}), bf16[1152,1076]{1,0:T(8,128)(2,1)}) %all-gather.5.cloned.1.call-update) | async-done | bytes 2479120 | tf_op jit(solution)/shard_map/all_gather | solution.py:214
  149.1 7.1 %convert_reduce_fusion.1 = (f32[1076]{0:T(1024)}, bf16[512,1076]{0,1:T(8,128)(2,1)S(1)}) fusion(f32[512,1076]{0,1:T(8,128)} %convolution_add_fusion, bf16[1152,1076]{1,0:T(8,128)(2,1)} %all-gather.5.cloned.1.call-done, f32[512,1152]{1,0:T(8,128)} %convolution_multiply_fusion), kind=kOutput, calls=%fused_computation.67 | convolution fusion | flops 1284213760 | bytes 8148176 | tf_op jit(solution)/shard_map/dot_general | solution.py:252
  157.2 3.4 convolution_convert_fusion.1
  166.4 4.2 %fusion.186 = f32[512,1152]{1,0:T(8,128)S(1)} fusion(bf16[512,1076]{0,1:T(8,128)(2,1)} %copy-done.78, bf16[1152,1076]{1,0:T(8,128)(2,1)} %all-gather.3.cloned.1.call-done), kind=kOutput, calls=%fused_computation.320 | convolution fusion | flops 1269301248 | bytes 5940224 | tf_op jit(solution)/shard_map/dot_general | solution.py:31
  177.8 12.4 %collective-permute-done.19 = bf16[256,1152]{1,0:T(8,128)(2,1)S(1)} collective-permute-done((bf16[256,1152]{1,0:T(8,128)(2,1)S(1)}, bf16[256,1152]{1,0:T(8,128)(2,1)S(1)}, u32[]{:S(2)}, u32[]{:S(2)}) %collective-permute-start.19) | collective-permute-done | bytes 589856 | tf_op jit(solution)/shard_map/ppermute | solution.py:169
  191.1 3.4 convolution_convert_fusion
  196.6 5.4 %collective-permute-done.14 = bf16[256,1152]{1,0:T(8,128)(2,1)} collective-permute-done((bf16[256,1152]{1,0:T(8,128)(2,1)S(1)}, bf16[256,1152]{1,0:T(8,128)(2,1)}, u32[]{:S(2)}, u32[]{:S(2)}) %collective-permute-start.14) | collective-permute-done | bytes 589856 | tf_op jit(solution)/shard_map/ppermute | solution.py:169
  226.2 6.7 %fusion.59 = f32[1152,864]{1,0:T(8,128)} fusion(bf16[512,864]{0,1:T(8,128)(2,1)} %copy-done.23, s32[1152]{0:T(1024)} %copy-done.59, f32[512,1152]{1,0:T(8,128)S(1)} %copy-done.7, f32[1152]{0:T(1024)} %copy-done.56, f32[1152]{0:T(1024)S(1)} %convert_element_type.268, f32[512]{0:T(512)S(1)} %copy-done.73, f32[512]{0:T(512)S(1)} %copy-done.55), kind=kOutput, calls=%fused_computation.136 | convolution fusion | flops 2383036416 | bytes 7243264 | tf_op jit(solution)/shard_map/dot_general | solution.py:31
  232.9 4.5 %fusion.55 = f32[1152,288]{1,0:T(8,128)S(1)} fusion(bf16[512,288]{0,1:T(8,128)(2,1)} %bitcast.128, s32[1152]{0:T(1024)} %copy-done.59, f32[512,1152]{1,0:T(8,128)} %copy-done.1), kind=kOutput, calls=%fused_computation.132 | convolution fusion | flops 1701199872 | bytes 3985920 | tf_op jit(solution)/shard_map/dot_general | solution.py:31
  254.5 12.0 %collective-permute-done.25 = bf16[144,1152]{1,0:T(8,128)(2,1)S(1)} collective-permute-done((bf16[144,1152]{1,0:T(8,128)(2,1)S(1)}, bf16[144,1152]{1,0:T(8,128)(2,1)S(1)}, u32[]{:S(2)}, u32[]{:S(2)}) %collective-permute-start.25) | collective-permute-done | bytes 331808 | tf_op jit(solution)/shard_map/ppermute | solution.py:133
  266.6 5.3 %collective-permute-start.26 = (bf16[144,1152]{1,0:T(8,128)(2,1)S(1)}, bf16[144,1152]{1,0:T(8,128)(2,1)S(1)}, u32[]{:S(2)}, u32[]{:S(2)}) collective-permute-start(bf16[144,1152]{1,0:T(8,128)(2,1)S(1)} %fusion.65), channel_id=1, source_target_pairs={{0,8},{8,16},{16,24},{24,28},{28,20},{20,12},{12,4},{4,0},{1,9},{9... | collective-permute-start | bytes 995336 | tf_op jit(solution)/shard_map/ppermute | solution.py:133
  274.8 8.4 %collective-permute-done.26 = bf16[144,1152]{1,0:T(8,128)(2,1)S(1)} collective-permute-done((bf16[144,1152]{1,0:T(8,128)(2,1)S(1)}, bf16[144,1152]{1,0:T(8,128)(2,1)S(1)}, u32[]{:S(2)}, u32[]{:S(2)}) %collective-permute-start.26) | collective-permute-done | bytes 331808 | tf_op jit(solution)/shard_map/ppermute | solution.py:133
  291.4 4.3 %collective-permute-done.30 = bf16[144,1152]{1,0:T(8,128)(2,1)} collective-permute-done((bf16[144,1152]{1,0:T(8,128)(2,1)}, bf16[144,1152]{1,0:T(8,128)(2,1)}, u32[]{:S(2)}, u32[]{:S(2)}) %collective-permute-start.30) | collective-permute-done | bytes 331808 | tf_op jit(solution)/shard_map/ppermute | solution.py:134
  302.8 12.4 %collective-permute-done.31 = bf16[144,1152]{1,0:T(8,128)(2,1)} collective-permute-done((bf16[144,1152]{1,0:T(8,128)(2,1)}, bf16[144,1152]{1,0:T(8,128)(2,1)}, u32[]{:S(2)}, u32[]{:S(2)}) %collective-permute-start.31) | collective-permute-done | bytes 331808 | tf_op jit(solution)/shard_map/ppermute | solution.py:134
  322.0 3.3 collective-permute-done.34
  325.4 4.2 %collective-permute-done.35 = f32[13520]{0:T(1024)S(1)} collective-permute-done((f32[13520]{0:T(1024)S(1)}, f32[13520]{0:T(1024)S(1)}, u32[]{:S(2)}, u32[]{:S(2)}) %collective-permute-start.35) | collective-permute-done | bytes 54112 | tf_op jit(solution)/shard_map/ppermute | solution.py:145
  (382 shorter events, 152.3 us)
Async XLA Ops:
  7.2 117.6 %all-gather.3.cloned.1.call-start = ((), (), s32[]{:S(2)}) async-start(), calls=%async_computation.2 | async-start | bytes 2985984 | tf_op jit(solution)/shard_map/all_gather | solution.py:213
  9.5 13.4 %collective-permute-start.2 = (bf16[144,1152]{1,0:T(8,128)(2,1)S(1)}, bf16[144,1152]{1,0:T(8,128)(2,1)S(1)}, u32[]{:S(2)}, u32[]{:S(2)}) collective-permute-start(bf16[144,1152]{1,0:T(8,128)(2,1)S(1)} %concatenate.45), channel_id=1, source_target_pairs={{8,0},{16,8},{24,16},{28,24},{20,28},{12,20},{4,12},{0,4},{9,1},{1... | collective-permute-start | bytes 995336 | tf_op jit(solution)/shard_map/ppermute | solution.py:102
  12.6 16.5 %collective-permute-start = (bf16[256,1152]{1,0:T(8,128)(2,1)}, bf16[256,1152]{1,0:T(8,128)(2,1)S(1)}, u32[]{:S(2)}, u32[]{:S(2)}) collective-permute-start(bf16[256,1152]{1,0:T(8,128)(2,1)} %bitcast.120), channel_id=1, source_target_pairs={{0,2},{1,3},{2,0},{3,1},{4,6},{5,7},{6,4},{7,5},{8,10},{9,11},{10,... | collective-permute-start | bytes 1769480 | tf_op jit(solution)/shard_map/ppermute | solution.py:154
  14.5 134.6 %all-gather.5.cloned.1.call-start = ((), (), s32[]{:S(2)}) async-start(), calls=%async_computation.3 | async-start | bytes 2985984 | tf_op jit(solution)/shard_map/all_gather | solution.py:214
  14.6 25.7 %collective-permute-start.16 = (bf16[256,1152]{1,0:T(8,128)(2,1)}, bf16[256,1152]{1,0:T(8,128)(2,1)S(1)}, u32[]{:S(2)}, u32[]{:S(2)}) collective-permute-start(bf16[256,1152]{1,0:T(8,128)(2,1)} %bitcast.136), channel_id=1, source_target_pairs={{0,2},{1,3},{2,0},{3,1},{4,6},{5,7},{6,4},{7,5},{8,10},{9,11},{10,... | collective-permute-start | bytes 1769480 | tf_op jit(solution)/shard_map/ppermute | solution.py:154
  22.9 17.5 %collective-permute-start.3 = (bf16[144,1152]{1,0:T(8,128)(2,1)S(1)}, bf16[144,1152]{1,0:T(8,128)(2,1)S(1)}, u32[]{:S(2)}, u32[]{:S(2)}) collective-permute-start(bf16[144,1152]{1,0:T(8,128)(2,1)S(1)} %collective-permute-done.2), channel_id=1, source_target_pairs={{8,0},{16,8},{24,16},{28,24},{20,28},{12,20},{4,12},{0,4},{9,1},{1... | collective-permute-start | bytes 995336 | tf_op jit(solution)/shard_map/ppermute | solution.py:102
  24.8 17.3 %collective-permute-start.6 = (bf16[144,1152]{1,0:T(8,128)(2,1)S(1)}, bf16[144,1152]{1,0:T(8,128)(2,1)S(1)}, u32[]{:S(2)}, u32[]{:S(2)}) collective-permute-start(bf16[144,1152]{1,0:T(8,128)(2,1)S(1)} %collective-permute-done.5), channel_id=1, source_target_pairs={{0,8},{8,16},{16,24},{24,28},{28,20},{20,12},{12,4},{4,0},{1,9},{9... | collective-permute-start | bytes 995336 | tf_op jit(solution)/shard_map/ppermute | solution.py:101
  29.4 48.7 %collective-permute-start.1 = (bf16[512,1152]{1,0:T(8,128)(2,1)S(1)}, bf16[512,1152]{1,0:T(8,128)(2,1)S(1)}, u32[]{:S(2)}, u32[]{:S(2)}) collective-permute-start(bf16[512,1152]{1,0:T(8,128)(2,1)S(1)} %pad_maximum_fusion.3), channel_id=1, source_target_pairs={{0,1},{1,0},{2,3},{3,2},{4,5},{5,4},{6,7},{7,6},{8,9},{9,8},{10,11... | collective-permute-start | bytes 3538952 | tf_op jit(solution)/shard_map/ppermute | solution.py:156
  44.2 58.2 %collective-permute-start.17 = (bf16[512,1152]{1,0:T(8,128)(2,1)}, bf16[512,1152]{1,0:T(8,128)(2,1)}, u32[]{:S(2)}, u32[]{:S(2)}) collective-permute-start(bf16[512,1152]{1,0:T(8,128)(2,1)} %pad_maximum_fusion.5), channel_id=1, source_target_pairs={{0,1},{1,0},{2,3},{3,2},{4,5},{5,4},{6,7},{7,6},{8,9},{9,8},{10,11... | collective-permute-start | bytes 3538952 | tf_op jit(solution)/shard_map/ppermute | solution.py:156
  52.0 21.9 %collective-permute-start.9 = (bf16[80,1152]{1,0:T(8,128)(2,1)S(1)}, bf16[80,1152]{1,0:T(8,128)(2,1)S(1)}, u32[]{:S(2)}, u32[]{:S(2)}) collective-permute-start(bf16[80,1152]{1,0:T(8,128)(2,1)S(1)} %slice.165), channel_id=1, source_target_pairs={{8,0},{16,8},{24,16},{28,24},{20,28},{12,20},{4,12},{0,4},{9,1},{1... | collective-permute-start | bytes 552968 | tf_op jit(solution)/shard_map/ppermute | solution.py:106
  92.7 243.9 %reduce-scatter.3.cloned.1.call-start = ((), (), s32[]{:S(2)}) async-start(), calls=%async_computation.4 | async-start | bytes 2985984 | tf_op jit(solution)/shard_map/reduce_scatter | solution.py:258
  99.6 16.8 %collective-permute-start.11 = (bf16[256,1152]{1,0:T(8,128)(2,1)S(1)}, bf16[256,1152]{1,0:T(8,128)(2,1)S(1)}, u32[]{:S(2)}, u32[]{:S(2)}) collective-permute-start(bf16[256,1152]{1,0:T(8,128)(2,1)S(1)} %add_convert_fusion.10), channel_id=1, source_target_pairs={{0,2},{1,3},{2,0},{3,1},{4,6},{5,7},{6,4},{7,5},{8,10},{9,11},{10,... | collective-permute-start | bytes 1769480 | tf_op jit(solution)/shard_map/ppermute | solution.py:169
  160.7 177.9 %reduce-scatter.5.cloned.1.call-start = ((), (), s32[]{:S(2)}) async-start(), calls=%async_computation.5 | async-start | bytes 2985984 | tf_op jit(solution)/shard_map/reduce_scatter | solution.py:256
  173.9 16.3 %collective-permute-start.19 = (bf16[256,1152]{1,0:T(8,128)(2,1)S(1)}, bf16[256,1152]{1,0:T(8,128)(2,1)S(1)}, u32[]{:S(2)}, u32[]{:S(2)}) collective-permute-start(bf16[256,1152]{1,0:T(8,128)(2,1)S(1)} %add_convert_fusion.6), channel_id=1, source_target_pairs={{0,2},{1,3},{2,0},{3,1},{4,6},{5,7},{6,4},{7,5},{8,10},{9,11},{10,... | collective-permute-start | bytes 1769480 | tf_op jit(solution)/shard_map/ppermute | solution.py:169
  177.2 24.8 %collective-permute-start.14 = (bf16[256,1152]{1,0:T(8,128)(2,1)S(1)}, bf16[256,1152]{1,0:T(8,128)(2,1)}, u32[]{:S(2)}, u32[]{:S(2)}) collective-permute-start(bf16[256,1152]{1,0:T(8,128)(2,1)S(1)} %add_convert_fusion.8), channel_id=1, source_target_pairs={{0,2},{1,3},{2,0},{3,1},{4,6},{5,7},{6,4},{7,5},{8,10},{9,11},{10,... | collective-permute-start | bytes 1769480 | tf_op jit(solution)/shard_map/ppermute | solution.py:169
  203.4 43.0 %collective-permute-start.15 = (bf16[256,1152]{1,0:T(8,128)(2,1)S(1)}, bf16[256,1152]{1,0:T(8,128)(2,1)}, u32[]{:S(2)}, u32[]{:S(2)}) collective-permute-start(bf16[256,1152]{1,0:T(8,128)(2,1)S(1)} %add_convert_fusion.7), channel_id=1, source_target_pairs={{0,1},{1,0},{2,3},{3,2},{4,5},{5,4},{6,7},{7,6},{8,9},{9,8},{10,11... | collective-permute-start | bytes 1769480 | tf_op jit(solution)/shard_map/ppermute | solution.py:171
  240.6 31.4 %collective-permute-start.21 = (bf16[256,1152]{1,0:T(8,128)(2,1)S(1)}, bf16[256,1152]{1,0:T(8,128)(2,1)S(1)}, u32[]{:S(2)}, u32[]{:S(2)}) collective-permute-start(bf16[256,1152]{1,0:T(8,128)(2,1)S(1)} %dynamic-slice_convert_fusion), channel_id=1, source_target_pairs={{0,1},{1,0},{2,3},{3,2},{4,5},{5,4},{6,7},{7,6},{8,9},{9,8},{10,11... | collective-permute-start | bytes 1769480 | tf_op jit(solution)/shard_map/ppermute | solution.py:167
  250.2 16.3 %collective-permute-start.25 = (bf16[144,1152]{1,0:T(8,128)(2,1)S(1)}, bf16[144,1152]{1,0:T(8,128)(2,1)S(1)}, u32[]{:S(2)}, u32[]{:S(2)}) collective-permute-start(bf16[144,1152]{1,0:T(8,128)(2,1)S(1)} %pad_maximum_fusion.9), channel_id=1, source_target_pairs={{0,8},{8,16},{16,24},{24,28},{28,20},{20,12},{12,4},{4,0},{1,9},{9... | collective-permute-start | bytes 995336 | tf_op jit(solution)/shard_map/ppermute | solution.py:133
  254.4 20.4 %collective-permute-start.29 = (bf16[144,1152]{1,0:T(8,128)(2,1)S(1)}, bf16[144,1152]{1,0:T(8,128)(2,1)S(1)}, u32[]{:S(2)}, u32[]{:S(2)}) collective-permute-start(bf16[144,1152]{1,0:T(8,128)(2,1)S(1)} %pad_maximum_fusion.10), channel_id=1, source_target_pairs={{8,0},{16,8},{24,16},{28,24},{20,28},{12,20},{4,12},{0,4},{9,1},{1... | collective-permute-start | bytes 995336 | tf_op jit(solution)/shard_map/ppermute | solution.py:134
  266.6 16.5 %collective-permute-start.26 = (bf16[144,1152]{1,0:T(8,128)(2,1)S(1)}, bf16[144,1152]{1,0:T(8,128)(2,1)S(1)}, u32[]{:S(2)}, u32[]{:S(2)}) collective-permute-start(bf16[144,1152]{1,0:T(8,128)(2,1)S(1)} %fusion.65), channel_id=1, source_target_pairs={{0,8},{8,16},{16,24},{24,28},{28,20},{20,12},{12,4},{4,0},{1,9},{9... | collective-permute-start | bytes 995336 | tf_op jit(solution)/shard_map/ppermute | solution.py:133
  284.9 15.3 %collective-permute-start.23 = (bf16[256,1152]{1,0:T(8,128)(2,1)S(1)}, bf16[256,1152]{1,0:T(8,128)(2,1)S(1)}, u32[]{:S(2)}, u32[]{:S(2)}) collective-permute-start(bf16[256,1152]{1,0:T(8,128)(2,1)S(1)} %add_convert_fusion.3), channel_id=1, source_target_pairs={{0,1},{1,0},{2,3},{3,2},{4,5},{5,4},{6,7},{7,6},{8,9},{9,8},{10,11... | collective-permute-start | bytes 1769480 | tf_op jit(solution)/shard_map/ppermute | solution.py:171
  288.2 14.6 %collective-permute-start.27 = (bf16[144,1152]{1,0:T(8,128)(2,1)}, bf16[144,1152]{1,0:T(8,128)(2,1)}, u32[]{:S(2)}, u32[]{:S(2)}) collective-permute-start(bf16[144,1152]{1,0:T(8,128)(2,1)} %get-tuple-element.86), channel_id=1, source_target_pairs={{0,8},{8,16},{16,24},{24,28},{28,20},{20,12},{12,4},{4,0},{1,9},{9... | collective-permute-start | bytes 995336 | tf_op jit(solution)/shard_map/ppermute | solution.py:133
  297.6 17.6 %collective-permute-start.31 = (bf16[144,1152]{1,0:T(8,128)(2,1)}, bf16[144,1152]{1,0:T(8,128)(2,1)}, u32[]{:S(2)}, u32[]{:S(2)}) collective-permute-start(bf16[144,1152]{1,0:T(8,128)(2,1)} %fusion.74), channel_id=1, source_target_pairs={{8,0},{16,8},{24,16},{28,24},{20,28},{12,20},{4,12},{0,4},{9,1},{1... | collective-permute-start | bytes 995336 | tf_op jit(solution)/shard_map/ppermute | solution.py:134
  302.8 14.0 %collective-permute-start.32 = (f32[13520]{0:T(1024)S(1)}, f32[13520]{0:T(1024)S(1)}, u32[]{:S(2)}, u32[]{:S(2)}) collective-permute-start(f32[13520]{0:T(1024)S(1)} %concatenate.57), channel_id=1, source_target_pairs={{0,1},{1,0},{2,3},{3,2},{4,5},{5,4},{6,7},{7,6},{8,9},{9,8},{10,11... | collective-permute-start | bytes 162248 | tf_op jit(solution)/shard_map/ppermute | solution.py:145
  (96 other events, 674.9 us)
Sparse Core Ops, SparseCore 0:
  14.7 62.5 all-gather.2
  92.9 56.1 all-gather.4
  160.8 69.3 reduce-scatter.2
  234.2 85.4 reduce-scatter.4

commit v2 on v1

--- a/solution.py
+++ b/solution.py
@@ -209,9 +209,9 @@
     attention_shard = jnp.concatenate(
         [joint_weight[0], joint_weight[1], joint_weight[2], out_weight.T], axis=1
     )
-    attention_full = ring_gather(attention_shard)
+    attention_full = lax.all_gather(attention_shard, "fsdp", axis=0, tiled=True)
     up_full = lax.all_gather(up_weight.T, "fsdp", axis=0, tiled=True)
-    down_full = lax.all_gather(down_weight.T, "fsdp", axis=0, tiled=True)
+    down_full = ring_gather(down_weight.T)
     joint_full = attention_full[:, : 3 * local_width]
     out_full = attention_full[:, 3 * local_width :]
 

time: 352 us -> 341 us (0.969)
  waiting for transfers between devices: 145 us -> 120 us
  local copies, waits for them, and re-layouts: 25.3 us -> 38.7 us
  matrix products: 72.7 us -> 76.7 us
    all_gather x1, waiting for transfers between devices: 19.4 us -> 0.01 us  [local(): attention_full = lax.all_gather(attention_shard, 'fsdp', axis=0, tiled=True)]
    all_gather x1, waiting for transfers between devices: 0.01 us -> 6.83 us  [local(): up_full = lax.all_gather(up_weight.T, 'fsdp', axis=0, tiled=True)]
    unnamed x172 -> x196, local copies, waits for them, and re-layouts: 10.2 us -> 17 us
    ppermute x1, waiting for transfers between devices: 13.6 us -> 7.1 us  [ring_gather(): bottom = lax.ppermute(second[cut:], 'fsdp', back)]
    ppermute x3, waiting for transfers between devices: 16.7 us -> 11.7 us  [ring_scatter(): second = lax.ppermute(second.astype(low), 'fsdp', back).astype(f32)]
    ppermute x1, starting transfers between devices: 0.56 us -> 4.46 us  [ring_gather(): top = lax.ppermute(first[:cut], 'fsdp', forth)]
    ppermute x3, starting transfers between devices: 10 us -> 6.45 us  [ring_scatter(): first = lax.ppermute(first.astype(low), 'fsdp', forth).astype(f32)]
    ppermute x3, waiting for transfers between devices: 7.18 us -> 10.7 us  [ring_gather(): first = lax.ppermute(first, 'fsdp', forth)]
  transfers between devices with their start and end apart: 41 -> 41, of which waited for: 18 -> 21; matrix products, arithmetic and copies ran while one was open for 36% -> 42% of each run, Pallas kernels for 0% -> 0%
where the time goes in v2:
time: 341 us; the launch traced here: 337 us
  waiting for transfers between devices  120 us (35%)
  matrix products  76.7 us (22%)
  other arithmetic  51.6 us (15%)
  local copies, waits for them, and re-layouts  38.7 us (11%)
  starting transfers between devices  34.5 us (10%)
  between operations  15.3 us (4%)
    dot_general x8, matrix products, contract(): lax.dot_general(former, latter, (((former_dim,), (latter_dim,)), ((), ())...  30.5 us
    ppermute x4, waiting for transfers between devices, sum_slots(): far = lax.ppermute(chip, 'tp', across)  26.9 us
    ppermute x3, waiting for transfers between devices, ring_scatter(): first = lax.ppermute(first.astype(low), 'fsdp', forth).astype(f32)  23.1 us
    unnamed x196, local copies, waits for them, and re-layouts  17 us
    ppermute x2, waiting for transfers between devices, gather_blocks(): far = lax.ppermute(block, 'tp', across)  13.1 us
    ppermute x5, waiting for transfers between devices, sum_everywhere(): values = values + lax.ppermute(values, axis, pairs)  11.9 us
    ppermute x3, waiting for transfers between devices, ring_scatter(): second = lax.ppermute(second.astype(low), 'fsdp', back).astype(f32)  11.7 us
    ppermute x3, waiting for transfers between devices, ring_gather(): first = lax.ppermute(first, 'fsdp', forth)  10.7 us
  transfers between devices with their start and end apart: 41, of which 21 were waited for; matrix products, arithmetic and copies ran while one was open for 42% of the time, Pallas kernels for 0%

profile of v2, /device:TPU:0, one launch (start us, length us, event | category | flops | bytes accessed | tf_op | source)
XLA Modules:
  0.0 337.3 jit_solution(18325348846271593940)
XLA Ops:
  30.3 10.9 %collective-permute-done.16 = bf16[256,1152]{1,0:T(8,128)(2,1)S(1)} collective-permute-done((bf16[256,1152]{1,0:T(8,128)(2,1)}, bf16[256,1152]{1,0:T(8,128)(2,1)S(1)}, u32[]{:S(2)}, u32[]{:S(2)}) %collective-permute-start.16) | collective-permute-done | bytes 589856 | tf_op jit(solution)/shard_map/ppermute | solution.py:154
  46.2 10.7 %collective-permute-done.10 = bf16[144,1076]{1,0:T(8,128)(2,1)S(1)} collective-permute-done((bf16[144,1076]{1,0:T(8,128)(2,1)S(1)}, bf16[144,1076]{1,0:T(8,128)(2,1)S(1)}, u32[]{:S(2)}, u32[]{:S(2)}) %collective-permute-start.10) | collective-permute-done | bytes 309920 | tf_op jit(solution)/shard_map/ppermute | solution.py:101
  57.0 4.5 %collective-permute-start.11 = (bf16[64,1076]{1,0:T(8,128)(2,1)S(1)}, bf16[64,1076]{1,0:T(8,128)(2,1)S(1)}, u32[]{:S(2)}, u32[]{:S(2)}) collective-permute-start(bf16[64,1076]{1,0:T(8,128)(2,1)S(1)} %slice.169), channel_id=1, source_target_pairs={{0,8},{8,16},{16,24},{24,28},{28,20},{20,12},{12,4},{4,0},{1,9},{9... | collective-permute-start | bytes 413192 | tf_op jit(solution)/shard_map/ppermute | solution.py:105
  64.2 4.9 %collective-permute-done.11 = bf16[64,1076]{1,0:T(8,128)(2,1)S(1)} collective-permute-done((bf16[64,1076]{1,0:T(8,128)(2,1)S(1)}, bf16[64,1076]{1,0:T(8,128)(2,1)S(1)}, u32[]{:S(2)}, u32[]{:S(2)}) %collective-permute-start.11) | collective-permute-done | bytes 137760 | tf_op jit(solution)/shard_map/ppermute | solution.py:105
  69.8 7.1 %collective-permute-done.12 = bf16[80,1076]{1,0:T(8,128)(2,1)S(1)} collective-permute-done((bf16[80,1076]{1,0:T(8,128)(2,1)S(1)}, bf16[80,1076]{1,0:T(8,128)(2,1)S(1)}, u32[]{:S(2)}, u32[]{:S(2)}) %collective-permute-start.12) | collective-permute-done | bytes 172192 | tf_op jit(solution)/shard_map/ppermute | solution.py:106
  100.2 5.4 %convolution_convert_fusion.2 = bf16[1152,1076]{0,1:T(8,128)(2,1)} fusion(bf16[1152,1076]{1,0:T(8,128)(2,1)S(1)} %copy-done.37, s32[1152]{0:T(1024)S(1)} %copy-done.59), kind=kOutput, calls=%fused_computation.11 | convolution fusion | flops 2858494464 | bytes 4962816 | tf_op jit(solution)/shard_map/dot_general | solution.py:108
  109.6 12.4 %collective-permute-done.3 = bf16[256,1152]{1,0:T(8,128)(2,1)S(1)} collective-permute-done((bf16[256,1152]{1,0:T(8,128)(2,1)S(1)}, bf16[256,1152]{1,0:T(8,128)(2,1)S(1)}, u32[]{:S(2)}, u32[]{:S(2)}) %collective-permute-start.3) | collective-permute-done | bytes 589856 | tf_op jit(solution)/shard_map/ppermute | solution.py:169
  129.0 6.8 %all-gather.5.cloned.1.call-done = bf16[1152,1076]{1,0:T(8,128)(2,1)} async-done(((bf16[144,1076]{1,0:T(8,128)(2,1)}), bf16[1152,1076]{1,0:T(8,128)(2,1)}) %all-gather.5.cloned.1.call-update) | async-done | bytes 2479120 | tf_op jit(solution)/shard_map/all_gather | solution.py:213
  135.8 3.7 %convolution_add_fusion = f32[512,1076]{0,1:T(8,128)S(1)} fusion(bf16[1152,1076]{1,0:T(8,128)(2,1)} %all-gather.5.cloned.1.call-done, f32[1076]{0:T(1024)S(1)} %copy-done.57, f32[512,1152]{1,0:T(8,128)S(1)} %get-tuple-element.83, f32[1152]{0:T(1024)S(1)} %copy-done.56, f32[1152]{0:T(1024)S(1)} %convert_element_type.288, f32[512]{0:T(512)S(1)} %fusion.147, ...), kind=kOutput, calls=%fused_computation.28 | convolution fusion | flops 1272801280 | bytes 7059664 | tf_op jit(solution)/shard_map/dot_general | solution.py:250
  139.6 4.1 %convert_reduce_fusion.1 = (f32[1076]{0:T(1024)}, bf16[512,1076]{0,1:T(8,128)(2,1)S(1)}) fusion(f32[512,1076]{0,1:T(8,128)S(1)} %convolution_add_fusion, bf16[1152,1076]{0,1:T(8,128)(2,1)S(1)} %copy-done.88, f32[512,1152]{1,0:T(8,128)S(1)} %copy-done.18), kind=kOutput, calls=%fused_computation.67 | convolution fusion | flops 1284213760 | bytes 8148176 | tf_op jit(solution)/shard_map/dot_general | solution.py:252
  144.6 3.5 %convolution_convert_fusion.1 = bf16[1152,1076]{1,0:T(8,128)(2,1)} fusion(bf16[512,1076]{0,1:T(8,128)(2,1)S(1)} %get-tuple-element.138, f32[512,1152]{1,0:T(8,128)S(1)} %get-tuple-element.83, f32[1152]{0:T(1024)S(1)} %copy-done.56, f32[1152]{0:T(1024)S(1)} %convert_element_type.288, f32[512]{0:T(512)S(1)} %fusion.147, f32[512]{0:T(512)S(1)} %broadcast_multiply_fusion), kind=kOutput, calls=%fused_computation.10 | convolution fusion | flops 1273489920 | bytes 5953536 | tf_op jit(solution)/shard_map/dot_general | solution.py:31
  154.9 4.1 %fusion.186 = f32[512,1152]{1,0:T(8,128)S(1)} fusion(bf16[512,1076]{0,1:T(8,128)(2,1)} %copy-done.90, bf16[1152,1076]{1,0:T(8,128)(2,1)} %all-gather.5.cloned.1.call-done), kind=kOutput, calls=%fused_computation.320 | convolution fusion | flops 1269301248 | bytes 5940224 | tf_op jit(solution)/shard_map/dot_general | solution.py:31
  165.7 3.4 convolution_convert_fusion
  171.3 9.4 %collective-permute-done.19 = bf16[256,1152]{1,0:T(8,128)(2,1)} collective-permute-done((bf16[256,1152]{1,0:T(8,128)(2,1)}, bf16[256,1152]{1,0:T(8,128)(2,1)}, u32[]{:S(2)}, u32[]{:S(2)}) %collective-permute-start.19) | collective-permute-done | bytes 589856 | tf_op jit(solution)/shard_map/ppermute | solution.py:169
  187.8 4.6 %collective-permute-done.14 = bf16[256,1152]{1,0:T(8,128)(2,1)} collective-permute-done((bf16[256,1152]{1,0:T(8,128)(2,1)S(1)}, bf16[256,1152]{1,0:T(8,128)(2,1)}, u32[]{:S(2)}, u32[]{:S(2)}) %collective-permute-start.14) | collective-permute-done | bytes 589856 | tf_op jit(solution)/shard_map/ppermute | solution.py:169
  214.1 4.5 %fusion.55 = f32[1152,288]{1,0:T(8,128)S(1)} fusion(bf16[512,288]{0,1:T(8,128)(2,1)S(1)} %bitcast.129, s32[1152]{0:T(1024)} %fusion.140, f32[512,1152]{1,0:T(8,128)} %copy-done.1), kind=kOutput, calls=%fused_computation.132 | convolution fusion | flops 1701199872 | bytes 3985920 | tf_op jit(solution)/shard_map/dot_general | solution.py:31
  223.0 7.4 %fusion.59 = f32[1152,864]{1,0:T(8,128)} fusion(bf16[512,864]{0,1:T(8,128)(2,1)} %constant_dynamic-update-slice_fusion.9, s32[1152]{0:T(1024)} %fusion.140, f32[512,1152]{1,0:T(8,128)} %copy-done.5, f32[1152]{0:T(1024)} %convert_element_type.269, f32[1152]{0:T(1024)S(1)} %convert_element_type.268, f32[512]{0:T(512)S(1)} %copy-done.80, f32[512]{0:T(512)S(1)} %copy-done.55), kind=kOutput, calls=%fused_computation.136 | convolution fusion | flops 2383036416 | bytes 7243264 | tf_op jit(solution)/shard_map/dot_general | solution.py:31
  252.2 8.8 %collective-permute-done.25 = bf16[144,1152]{1,0:T(8,128)(2,1)S(1)} collective-permute-done((bf16[144,1152]{1,0:T(8,128)(2,1)S(1)}, bf16[144,1152]{1,0:T(8,128)(2,1)S(1)}, u32[]{:S(2)}, u32[]{:S(2)}) %collective-permute-start.25) | collective-permute-done | bytes 331808 | tf_op jit(solution)/shard_map/ppermute | solution.py:133
  265.4 11.0 %collective-permute-done.26 = bf16[144,1152]{1,0:T(8,128)(2,1)S(1)} collective-permute-done((bf16[144,1152]{1,0:T(8,128)(2,1)S(1)}, bf16[144,1152]{1,0:T(8,128)(2,1)S(1)}, u32[]{:S(2)}, u32[]{:S(2)}) %collective-permute-start.26) | collective-permute-done | bytes 331808 | tf_op jit(solution)/shard_map/ppermute | solution.py:133
  283.1 5.4 %collective-permute-done.30 = bf16[144,1152]{1,0:T(8,128)(2,1)} collective-permute-done((bf16[144,1152]{1,0:T(8,128)(2,1)}, bf16[144,1152]{1,0:T(8,128)(2,1)}, u32[]{:S(2)}, u32[]{:S(2)}) %collective-permute-start.30) | collective-permute-done | bytes 331808 | tf_op jit(solution)/shard_map/ppermute | solution.py:134
  295.0 3.3 collective-permute-done.27
  298.3 6.2 %collective-permute-done.31 = bf16[144,1152]{1,0:T(8,128)(2,1)} collective-permute-done((bf16[144,1152]{1,0:T(8,128)(2,1)}, bf16[144,1152]{1,0:T(8,128)(2,1)}, u32[]{:S(2)}, u32[]{:S(2)}) %collective-permute-start.31) | collective-permute-done | bytes 331808 | tf_op jit(solution)/shard_map/ppermute | solution.py:134
  311.3 3.3 collective-permute-done.34
  315.3 3.8 %collective-permute-done.35 = f32[13520]{0:T(1024)S(1)} collective-permute-done((f32[13520]{0:T(1024)S(1)}, f32[13520]{0:T(1024)S(1)}, u32[]{:S(2)}, u32[]{:S(2)}) %collective-permute-start.35) | collective-permute-done | bytes 54112 | tf_op jit(solution)/shard_map/ppermute | solution.py:145
  (406 shorter events, 172.6 us)
Async XLA Ops:
  7.3 77.0 %all-gather.3.cloned.1.call-start = ((), (), s32[]{:S(2)}) async-start(), calls=%async_computation.2 | async-start | bytes 2985984 | tf_op jit(solution)/shard_map/all_gather | solution.py:212
  10.4 125.4 %all-gather.5.cloned.1.call-start = ((), (), s32[]{:S(2)}) async-start(), calls=%async_computation.3 | async-start | bytes 2985984 | tf_op jit(solution)/shard_map/all_gather | solution.py:213
  10.4 14.6 %collective-permute-start.5 = (bf16[144,1076]{1,0:T(8,128)(2,1)}, bf16[144,1076]{1,0:T(8,128)(2,1)S(1)}, u32[]{:S(2)}, u32[]{:S(2)}) collective-permute-start(bf16[144,1076]{1,0:T(8,128)(2,1)} %bitcast.138), channel_id=1, source_target_pairs={{8,0},{16,8},{24,16},{28,24},{20,28},{12,20},{4,12},{0,4},{9,1},{1... | collective-permute-start | bytes 929672 | tf_op jit(solution)/shard_map/ppermute | solution.py:102
  13.5 16.5 %collective-permute-start = (bf16[256,1152]{1,0:T(8,128)(2,1)}, bf16[256,1152]{1,0:T(8,128)(2,1)S(1)}, u32[]{:S(2)}, u32[]{:S(2)}) collective-permute-start(bf16[256,1152]{1,0:T(8,128)(2,1)} %bitcast.121), channel_id=1, source_target_pairs={{0,2},{1,3},{2,0},{3,1},{4,6},{5,7},{6,4},{7,5},{8,10},{9,11},{10,... | collective-permute-start | bytes 1769480 | tf_op jit(solution)/shard_map/ppermute | solution.py:154
  15.4 25.8 %collective-permute-start.16 = (bf16[256,1152]{1,0:T(8,128)(2,1)}, bf16[256,1152]{1,0:T(8,128)(2,1)S(1)}, u32[]{:S(2)}, u32[]{:S(2)}) collective-permute-start(bf16[256,1152]{1,0:T(8,128)(2,1)} %bitcast.137), channel_id=1, source_target_pairs={{0,2},{1,3},{2,0},{3,1},{4,6},{5,7},{6,4},{7,5},{8,10},{9,11},{10,... | collective-permute-start | bytes 1769480 | tf_op jit(solution)/shard_map/ppermute | solution.py:154
  15.6 311.2 %reduce-scatter.3.cloned.1.call-start = ((), (), s32[]{:S(2)}) async-start(), calls=%async_computation.4 | async-start | bytes 2985984 | tf_op jit(solution)/shard_map/reduce_scatter | solution.py:258
  25.0 17.3 %collective-permute-start.6 = (bf16[144,1076]{1,0:T(8,128)(2,1)S(1)}, bf16[144,1076]{1,0:T(8,128)(2,1)S(1)}, u32[]{:S(2)}, u32[]{:S(2)}) collective-permute-start(bf16[144,1076]{1,0:T(8,128)(2,1)S(1)} %collective-permute-done.5), channel_id=1, source_target_pairs={{8,0},{16,8},{24,16},{28,24},{20,28},{12,20},{4,12},{0,4},{9,1},{1... | collective-permute-start | bytes 929672 | tf_op jit(solution)/shard_map/ppermute | solution.py:102
  26.9 16.1 %collective-permute-start.9 = (bf16[144,1076]{1,0:T(8,128)(2,1)S(1)}, bf16[144,1076]{1,0:T(8,128)(2,1)S(1)}, u32[]{:S(2)}, u32[]{:S(2)}) collective-permute-start(bf16[144,1076]{1,0:T(8,128)(2,1)S(1)} %collective-permute-done.8), channel_id=1, source_target_pairs={{0,8},{8,16},{16,24},{24,28},{28,20},{20,12},{12,4},{4,0},{1,9},{9... | collective-permute-start | bytes 929672 | tf_op jit(solution)/shard_map/ppermute | solution.py:101
  30.2 49.6 %collective-permute-start.1 = (bf16[512,1152]{1,0:T(8,128)(2,1)S(1)}, bf16[512,1152]{1,0:T(8,128)(2,1)S(1)}, u32[]{:S(2)}, u32[]{:S(2)}) collective-permute-start(bf16[512,1152]{1,0:T(8,128)(2,1)S(1)} %pad_maximum_fusion.3), channel_id=1, source_target_pairs={{0,1},{1,0},{2,3},{3,2},{4,5},{5,4},{6,7},{7,6},{8,9},{9,8},{10,11... | collective-permute-start | bytes 3538952 | tf_op jit(solution)/shard_map/ppermute | solution.py:156
  42.3 19.1 %collective-permute-start.7 = (bf16[144,1076]{1,0:T(8,128)(2,1)S(1)}, bf16[144,1076]{1,0:T(8,128)(2,1)S(1)}, u32[]{:S(2)}, u32[]{:S(2)}) collective-permute-start(bf16[144,1076]{1,0:T(8,128)(2,1)S(1)} %collective-permute-done.6), channel_id=1, source_target_pairs={{8,0},{16,8},{24,16},{28,24},{20,28},{12,20},{4,12},{0,4},{9,1},{1... | collective-permute-start | bytes 929672 | tf_op jit(solution)/shard_map/ppermute | solution.py:102
  43.0 13.9 %collective-permute-start.10 = (bf16[144,1076]{1,0:T(8,128)(2,1)S(1)}, bf16[144,1076]{1,0:T(8,128)(2,1)S(1)}, u32[]{:S(2)}, u32[]{:S(2)}) collective-permute-start(bf16[144,1076]{1,0:T(8,128)(2,1)S(1)} %collective-permute-done.9), channel_id=1, source_target_pairs={{0,8},{8,16},{16,24},{24,28},{28,20},{20,12},{12,4},{4,0},{1,9},{9... | collective-permute-start | bytes 929672 | tf_op jit(solution)/shard_map/ppermute | solution.py:101
  45.5 62.3 %collective-permute-start.17 = (bf16[512,1152]{1,0:T(8,128)(2,1)}, bf16[512,1152]{1,0:T(8,128)(2,1)}, u32[]{:S(2)}, u32[]{:S(2)}) collective-permute-start(bf16[512,1152]{1,0:T(8,128)(2,1)} %pad_maximum_fusion.5), channel_id=1, source_target_pairs={{0,1},{1,0},{2,3},{3,2},{4,5},{5,4},{6,7},{7,6},{8,9},{9,8},{10,11... | collective-permute-start | bytes 3538952 | tf_op jit(solution)/shard_map/ppermute | solution.py:156
  61.4 15.4 %collective-permute-start.12 = (bf16[80,1076]{1,0:T(8,128)(2,1)S(1)}, bf16[80,1076]{1,0:T(8,128)(2,1)S(1)}, u32[]{:S(2)}, u32[]{:S(2)}) collective-permute-start(bf16[80,1076]{1,0:T(8,128)(2,1)S(1)} %slice.170), channel_id=1, source_target_pairs={{8,0},{16,8},{24,16},{28,24},{20,28},{12,20},{4,12},{0,4},{9,1},{1... | collective-permute-start | bytes 516488 | tf_op jit(solution)/shard_map/ppermute | solution.py:106
  106.2 15.8 %collective-permute-start.3 = (bf16[256,1152]{1,0:T(8,128)(2,1)S(1)}, bf16[256,1152]{1,0:T(8,128)(2,1)S(1)}, u32[]{:S(2)}, u32[]{:S(2)}) collective-permute-start(bf16[256,1152]{1,0:T(8,128)(2,1)S(1)} %add_convert_fusion.10), channel_id=1, source_target_pairs={{0,2},{1,3},{2,0},{3,1},{4,6},{5,7},{6,4},{7,5},{8,10},{9,11},{10,... | collective-permute-start | bytes 1769480 | tf_op jit(solution)/shard_map/ppermute | solution.py:169
  148.1 180.5 %reduce-scatter.5.cloned.1.call-start = ((), (), s32[]{:S(2)}) async-start(), calls=%async_computation.5 | async-start | bytes 2985984 | tf_op jit(solution)/shard_map/reduce_scatter | solution.py:256
  164.2 16.5 %collective-permute-start.19 = (bf16[256,1152]{1,0:T(8,128)(2,1)}, bf16[256,1152]{1,0:T(8,128)(2,1)}, u32[]{:S(2)}, u32[]{:S(2)}) collective-permute-start(bf16[256,1152]{1,0:T(8,128)(2,1)} %add_convert_fusion.6), channel_id=1, source_target_pairs={{0,2},{1,3},{2,0},{3,1},{4,6},{5,7},{6,4},{7,5},{8,10},{9,11},{10,... | collective-permute-start | bytes 1769480 | tf_op jit(solution)/shard_map/ppermute | solution.py:169
  170.7 21.7 %collective-permute-start.14 = (bf16[256,1152]{1,0:T(8,128)(2,1)S(1)}, bf16[256,1152]{1,0:T(8,128)(2,1)}, u32[]{:S(2)}, u32[]{:S(2)}) collective-permute-start(bf16[256,1152]{1,0:T(8,128)(2,1)S(1)} %add_convert_fusion.8), channel_id=1, source_target_pairs={{0,2},{1,3},{2,0},{3,1},{4,6},{5,7},{6,4},{7,5},{8,10},{9,11},{10,... | collective-permute-start | bytes 1769480 | tf_op jit(solution)/shard_map/ppermute | solution.py:169
  193.8 48.4 %collective-permute-start.15 = (bf16[256,1152]{1,0:T(8,128)(2,1)S(1)}, bf16[256,1152]{1,0:T(8,128)(2,1)}, u32[]{:S(2)}, u32[]{:S(2)}) collective-permute-start(bf16[256,1152]{1,0:T(8,128)(2,1)S(1)} %add_convert_fusion.7), channel_id=1, source_target_pairs={{0,1},{1,0},{2,3},{3,2},{4,5},{5,4},{6,7},{7,6},{8,9},{9,8},{10,11... | collective-permute-start | bytes 1769480 | tf_op jit(solution)/shard_map/ppermute | solution.py:171
  236.7 27.0 %collective-permute-start.21 = (bf16[256,1152]{1,0:T(8,128)(2,1)S(1)}, bf16[256,1152]{1,0:T(8,128)(2,1)S(1)}, u32[]{:S(2)}, u32[]{:S(2)}) collective-permute-start(bf16[256,1152]{1,0:T(8,128)(2,1)S(1)} %dynamic-slice_convert_fusion), channel_id=1, source_target_pairs={{0,1},{1,0},{2,3},{3,2},{4,5},{5,4},{6,7},{7,6},{8,9},{9,8},{10,11... | collective-permute-start | bytes 1769480 | tf_op jit(solution)/shard_map/ppermute | solution.py:167
  246.5 14.5 %collective-permute-start.25 = (bf16[144,1152]{1,0:T(8,128)(2,1)S(1)}, bf16[144,1152]{1,0:T(8,128)(2,1)S(1)}, u32[]{:S(2)}, u32[]{:S(2)}) collective-permute-start(bf16[144,1152]{1,0:T(8,128)(2,1)S(1)} %pad_maximum_fusion.9), channel_id=1, source_target_pairs={{0,8},{8,16},{16,24},{24,28},{28,20},{20,12},{12,4},{4,0},{1,9},{9... | collective-permute-start | bytes 995336 | tf_op jit(solution)/shard_map/ppermute | solution.py:133
  261.2 15.3 %collective-permute-start.26 = (bf16[144,1152]{1,0:T(8,128)(2,1)S(1)}, bf16[144,1152]{1,0:T(8,128)(2,1)S(1)}, u32[]{:S(2)}, u32[]{:S(2)}) collective-permute-start(bf16[144,1152]{1,0:T(8,128)(2,1)S(1)} %fusion.68), channel_id=1, source_target_pairs={{0,8},{8,16},{16,24},{24,28},{28,20},{20,12},{12,4},{4,0},{1,9},{9... | collective-permute-start | bytes 995336 | tf_op jit(solution)/shard_map/ppermute | solution.py:133
  263.8 14.3 %collective-permute-start.22 = (bf16[256,1152]{1,0:T(8,128)(2,1)S(1)}, bf16[256,1152]{1,0:T(8,128)(2,1)S(1)}, u32[]{:S(2)}, u32[]{:S(2)}) collective-permute-start(bf16[256,1152]{1,0:T(8,128)(2,1)S(1)} %add_convert_fusion.4), channel_id=1, source_target_pairs={{0,2},{1,3},{2,0},{3,1},{4,6},{5,7},{6,4},{7,5},{8,10},{9,11},{10,... | collective-permute-start | bytes 1769480 | tf_op jit(solution)/shard_map/ppermute | solution.py:169
  281.6 16.8 %collective-permute-start.27 = (bf16[144,1152]{1,0:T(8,128)(2,1)}, bf16[144,1152]{1,0:T(8,128)(2,1)}, u32[]{:S(2)}, u32[]{:S(2)}) collective-permute-start(bf16[144,1152]{1,0:T(8,128)(2,1)} %get-tuple-element.86), channel_id=1, source_target_pairs={{0,8},{8,16},{16,24},{24,28},{28,20},{20,12},{12,4},{4,0},{1,9},{9... | collective-permute-start | bytes 995336 | tf_op jit(solution)/shard_map/ppermute | solution.py:133
  290.5 14.1 %collective-permute-start.31 = (bf16[144,1152]{1,0:T(8,128)(2,1)}, bf16[144,1152]{1,0:T(8,128)(2,1)}, u32[]{:S(2)}, u32[]{:S(2)}) collective-permute-start(bf16[144,1152]{1,0:T(8,128)(2,1)} %fusion.77), channel_id=1, source_target_pairs={{8,0},{16,8},{24,16},{28,24},{20,28},{12,20},{4,12},{0,4},{9,1},{1... | collective-permute-start | bytes 995336 | tf_op jit(solution)/shard_map/ppermute | solution.py:134
  (108 other events, 767.6 us)
Sparse Core Ops, SparseCore 0:
  10.9 66.5 all-gather.2
  79.7 56.0 all-gather.4
  148.3 69.0 reduce-scatter.2
  221.3 83.7 reduce-scatter.4
